TPU v7x, 32 devices: a whole 2x2x4 slice. The times are simulated.
32 devices in a mesh: slab: 16 (over z, y, x), dp: 2 (over core).
Axes of the slice: x: 2, y: 2, z: 4, core: 2. Of those that a mesh axis runs over, the one named last changes fastest.
Arguments:
- field: bfloat16 [2, 64, 32, 64, 512], P('dp', 'slab'), may hold values from -6 to 6
- cotangent: bfloat16 [2, 64, 32, 64, 512], P('dp', 'slab'), may hold values from -6 to 6
- spectral_weight: bfloat16 [96, 16, 16, 32, 64], P('slab'), may hold values from -9 to 9
- point_weight: bfloat16 [32, 32], replicated, may hold values from -1 to 1
- bias_term: float32 [32], replicated, may hold values from -3 to 3
Outputs:
- layer_out: bfloat16 [2, 64, 32, 64, 512], P('dp', 'slab')
- field_grad: bfloat16 [2, 64, 32, 64, 512], P('dp', 'slab')
- weight_grad: float32 [96, 16, 16, 32, 64], P('slab')
All inputs are finite; a program needn't handle non-finite values.
Results may differ from a plain program's by a relative error of at most 0.018.
Values may be sent and summed in bfloat16 or wider, within the bound.
A program may use at most 192 MiB of HBM per device.

v0:
```python
from functools import partial
import math

import jax
import jax.numpy as jnp
from jax import lax
from jax.sharding import PartitionSpec as P

X = 64
Y = 64
Z = 32
T_SIZE = 16
MX = 16
MY = 16
MZ = 12
MT = 8


def signed_freq(index, modes):
    return jnp.where(index < modes // 2, index, index - modes)


def inner_table():
    freq = jnp.arange(MZ * MT, dtype=jnp.int32)
    place = jnp.arange(Z * T_SIZE, dtype=jnp.int32)
    kdepth = (signed_freq(freq // MT, MZ) % Z)[:, None]
    ktime = (freq % MT)[:, None]
    zdepth = (place // T_SIZE)[None, :]
    tlevel = (place % T_SIZE)[None, :]
    counts = kdepth * zdepth % Z * T_SIZE + ktime * tlevel % T_SIZE * Z
    angle = 2.0 * math.pi / (Z * T_SIZE) * (counts % (Z * T_SIZE)).astype(jnp.float32)
    return jnp.stack([jnp.cos(angle), -jnp.sin(angle)]).astype(jnp.bfloat16)


def complex_table(modes, length):
    kpos = (signed_freq(jnp.arange(modes, dtype=jnp.int32), modes) % length)[:, None]
    jpos = jnp.arange(length, dtype=jnp.int32)[None, :]
    angle = 2.0 * math.pi / length * (kpos * jpos % length).astype(jnp.float32)
    cosine = jnp.cos(angle)
    sine = jnp.sin(angle)
    first = jnp.stack([cosine, sine], axis=1)
    second = jnp.stack([-sine, cosine], axis=1)
    return jnp.stack([first, second]).astype(jnp.bfloat16)


def contract(form, left, right):
    return jnp.einsum(form, left, right, preferred_element_type=jnp.float32)


def analyse(values, inner, middle, outer):
    first = contract("xcyt,pqt->xqpyc", values, inner).astype(jnp.bfloat16)
    second = contract("rkpy,xqpyc->xqrkc", middle, first).astype(jnp.bfloat16)
    second = lax.all_to_all(second, "slab", split_axis=1, concat_axis=0, tiled=True)
    return contract("rkpx,xqpyc->qkryc", outer, second)


def synthesise(spectrum, inner, middle, outer):
    first = contract("pkrx,qkpyc->xqryc", outer, spectrum).astype(jnp.bfloat16)
    first = lax.all_to_all(first, "slab", split_axis=0, concat_axis=1, tiled=True)
    second = contract("pkry,xqpkc->xqryc", middle, first).astype(jnp.bfloat16)
    return contract("xqpyc,pqt->xcyt", second, inner)


def pairs(grad_spec):
    real_part = grad_spec[..., 0, :, :]
    imag_part = grad_spec[..., 1, :, :]
    first = jnp.concatenate([real_part, imag_part], axis=-1)
    second = jnp.concatenate([imag_part, -real_part], axis=-1)
    return jnp.stack([first, second], axis=-3)


def mixing(spectrum, weights):
    width = spectrum.shape[-1]
    both = contract("qkpyc,qkyco->qkpyo", spectrum, weights)
    real_part = both[:, :, 0, :, :width] - both[:, :, 1, :, width:]
    imag_part = both[:, :, 0, :, width:] + both[:, :, 1, :, :width]
    return jnp.stack([real_part, imag_part], axis=2).astype(jnp.bfloat16)


def add_samples(pieces):
    spec_piece, grad_piece = pieces
    return contract("sqkpyc,sqkpyo->qkyco", spec_piece, pairs(grad_piece))


def per_device(field, cotangent, spectral_weight, point_weight, bias_term):
    inputs = field[0]
    upstream = cotangent[0]
    inner = inner_table()
    middle = complex_table(MY, Y)
    outer = complex_table(MX, X)
    scale = 1.0 / (X * Y * Z * T_SIZE)
    spectrum = analyse(inputs, inner, middle, outer).astype(jnp.bfloat16)
    mixed = mixing(spectrum, spectral_weight)
    spectral = synthesise(mixed, inner, middle, outer) * scale
    linear = contract("oc,xcyt->xoyt", point_weight, inputs)
    preact = spectral + linear + bias_term[None, :, None, None]
    activation = partial(jax.nn.gelu, approximate=True)
    layer_out = activation(preact).astype(jnp.bfloat16)
    pulled = jax.vjp(activation, preact)[1](upstream.astype(jnp.float32))[0]
    grad_pre = pulled.astype(jnp.bfloat16)
    grad_spec = (analyse(grad_pre, inner, middle, outer) * scale).astype(jnp.bfloat16)
    paired = pairs(grad_spec)
    weight_grad = add_samples(
        (
            lax.all_gather(spectrum[None], "dp", axis=0, tiled=True),
            lax.all_gather(grad_spec[None], "dp", axis=0, tiled=True),
        )
    )
    spec_back = contract("qkyco,qkpyo->qkpyc", spectral_weight, paired).astype(jnp.bfloat16)
    total = synthesise(spec_back, inner, middle, outer) + contract(
        "oc,xoyt->xcyt", point_weight, grad_pre
    )
    return (layer_out[None], total.astype(jnp.bfloat16)[None], weight_grad)


def solution(mesh):
    placed = (
        P("dp", "slab", None, None, None),
        P("dp", "slab", None, None, None),
        P("slab", None, None, None, None),
        P(),
        P(),
    )
    return jax.shard_map(
        per_device,
        mesh=mesh,
        in_specs=placed,
        out_specs=(
            P("dp", "slab", None, None, None),
            P("dp", "slab", None, None, None),
            P("slab", None, None, None, None),
        ),
        check_vma=False,
    )
```

profile of v0, /device:TPU:0, one launch (start us, length us, event | category | flops | bytes accessed | tf_op | source)
XLA Modules:
  0.0 287.1 jit_solution(7408535736679648064)
XLA Ops:
  0.8 1.0 cosine_convert_fusion
  1.9 6.4 %fusion.67 = bf16[4,96,2,16,32]{1,3,2,4,0:T(8,128)(2,1)} fusion(bf16[1,4,32,64,512]{4,3,2,1,0:T(8,128)(2,1)} %param.5, bf16[1,96,512]{2,1,0:T(8,128)(2,1)S(1)} %get-tuple-element.16, bf16[1,96,512]{2,1,0:T(8,128)(2,1)S(1)} %get-tuple-element.15, bf16[1,16,2,64]{3,1,2,0:T(8,128)(2,1)S(1)} %get-tuple-element.18, bf16[1,16,2,64]{3,1,2,0:T(8,128)(2,1)S(1)} %get-tuple-element.17), kind=kOutput, calls=%fused_computation.62 | convolution fusion | flops 1713651712 | bytes 9379840 | tf_op jit(solution)/shard_map/rkpy,xqpyc->xqrkc/dot_general | solution.py:47
  8.2 6.4 %copy.117 = bf16[4,96,2,16,32]{4,3,2,0,1:T(8,128)(2,1)S(1)} copy(bf16[4,96,2,16,32]{1,3,2,4,0:T(8,128)(2,1)} %fusion.67) | data formatting | bytes 1572864 | tf_op jit(solution)/shard_map/convert_element_type | solution.py:52
  14.6 3.7 %reshape.524 = bf16[16,2,12288]{2,1,0:T(2,128)(2,1)} reshape(bf16[96,4,2,16,32]{4,3,2,1,0:T(8,128)(2,1)S(1)} %bitcast.283) | data formatting | bytes 1572864
  18.3 29.9 %all_to_all.72 = bf16[16,2,12288]{2,1,0:T(2,128)(2,1)} all-to-all(bf16[16,2,12288]{2,1,0:T(2,128)(2,1)} %reshape.524), channel_id=1, replica_groups=mesh['slab'=16,'dp'=2] {'slab'}, dimensions={0} | all-to-all | bytes 1572864 | tf_op jit(solution)/shard_map/all_to_all | solution.py:53
  48.3 3.9 %reshape.525 = bf16[96,4,2,16,32]{4,3,2,1,0:T(8,128)(2,1)S(1)} reshape(bf16[16,2,12288]{2,1,0:T(2,128)(2,1)} %all_to_all.72) | data formatting | bytes 1572864
  52.2 0.9 copy.119
  53.1 2.0 fusion.78
  55.2 6.6 %convolution_bitcast_fusion.1 = f32[6,16,2,16,64]{4,2,3,1,0:T(2,128)S(1)} fusion(bf16[6,16,16,32,64]{4,3,2,1,0:T(8,128)(2,1)} %param.7, bf16[6,16,2,16,32]{4,1,2,3,0:T(8,128)(2,1)S(1)} %fusion.78), kind=kOutput, calls=%fused_computation.58 | convolution fusion | flops 12582912 | bytes 7274496 | tf_op jit(solution)/shard_map/qkpyc,qkyco->qkpyo/dot_general | solution.py:47
  61.8 3.4 %fusion.85 = (bf16[6,16,1,16,32]{4,2,3,1,0:T(2,128)(2,1)S(1)}, bf16[6,16,1,16,32]{4,2,3,1,0:T(2,128)(2,1)S(1)}) fusion(f32[6,16,2,16,64]{4,2,3,1,0:T(2,128)S(1)} %convolution_bitcast_fusion.1), kind=kLoop, calls=%fused_computation.70 | loop fusion | flops 196608 | bytes 983040 | tf_op jit(solution)/shard_map/convert.1
  65.2 2.1 maximum_bitcast_fusion
  67.3 1.8 fusion.65
  69.1 7.2 %copy.124 = bf16[64,6,2,16,32]{4,2,3,1,0:T(2,128)(2,1)S(1)} copy(bf16[64,6,2,16,32]{0,4,2,3,1:T(8,128)(2,1)} %fusion.65) | data formatting | bytes 1572864 | tf_op jit(solution)/shard_map/convert_element_type | solution.py:58
  76.3 3.7 %reshape.526 = bf16[16,2,12288]{2,1,0:T(2,128)(2,1)} reshape(bf16[64,6,16,2,32]{4,3,2,1,0:T(2,128)(2,1)S(1)} %bitcast.278) | data formatting | bytes 1572864
  80.0 4.7 %all-to-all-start.1 = ((bf16[16,2,12288]{2,1,0:T(2,128)(2,1)}), bf16[16,2,12288]{2,1,0:T(2,128)(2,1)}, u32[]{:S(2)}, u32[]{:S(2)}) async-start(bf16[16,2,12288]{2,1,0:T(2,128)(2,1)} %reshape.526), calls=%async_computation.1 | async-start | bytes 1572864 | tf_op jit(solution)/shard_map/all_to_all | solution.py:59
  84.8 16.2 %fusion.18 = f32[4,64,512,32]{2,3,1,0:T(8,128)} fusion(bf16[4,32,64,512]{3,2,1,0:T(8,128)(2,1)} %bitcast.285, bf16[32,32]{1,0:T(8,128)(2,1)S(1)} %copy-done), kind=kOutput, calls=%fused_computation.29 | convolution fusion | flops 268435456 | bytes 25167872 | tf_op jit(solution)/shard_map/oc,xcyt->xoyt/dot_general | solution.py:47
  100.9 1.2 copy.147
  102.1 1.1 all-to-all-done.1
  103.3 7.2 %reshape.527 = bf16[64,6,16,2,32]{4,3,2,1,0:T(2,128)(2,1)S(1)} reshape(bf16[16,2,12288]{2,1,0:T(2,128)(2,1)} %all-to-all-done.1) | data formatting | bytes 1572864
  110.5 0.6 copy.125
  111.1 0.7 copy.126
  111.8 4.8 %copy.163 = bf16[4,96,2,16,32,1]{1,3,2,5,4,0:T(8,128)(2,1)} copy(bf16[4,96,2,16,32,1]{4,3,2,1,0,5:T(8,128)(2,1)S(1)} %bitcast.274) | data formatting | bytes 1572864 | tf_op jit(solution)/shard_map/all_to_all | solution.py:59
  116.6 27.6 %fusion.2 = (bf16[4,32,64,512]{3,2,1,0:T(8,128)(2,1)}, bf16[1,4,32,64,512]{4,3,2,1,0:T(8,128)(2,1)}) fusion(bf16[1,4,32,64,512]{4,3,2,1,0:T(8,128)(2,1)} %param.6, f32[32]{0:T(128)S(1)} %copy-done.4, f32[4,64,512,32]{2,3,1,0:T(8,128)} %fusion.18, bf16[4,96,2,16,32,1]{1,3,2,5,4,0:T(8,128)(2,1)} %copy.163, bf16[1,96,512]{2,1,0:T(8,128)(2,1)S(1)} %get-tuple-element.16, ...), kind=kOutput, calls=%fused_computation.6 | convolution fusion | flops 1822298112 | bytes 42934400 | tf_op jit(solution)/shard_map/xqpyc,pqt->xcyt/dot_general | solution.py:47
  144.2 6.3 %fusion.72 = bf16[4,96,2,16,32]{1,3,2,4,0:T(8,128)(2,1)} fusion(bf16[4,32,64,512]{3,2,1,0:T(8,128)(2,1)} %get-tuple-element.3, bf16[1,96,512]{2,1,0:T(8,128)(2,1)S(1)} %get-tuple-element.16, bf16[1,96,512]{2,1,0:T(8,128)(2,1)S(1)} %get-tuple-element.15, bf16[1,16,2,64]{3,1,2,0:T(8,128)(2,1)S(1)} %get-tuple-element.18, ...), kind=kOutput, calls=%fused_computation.63 | convolution fusion | flops 1713651712 | bytes 9379840 | tf_op jit(solution)/shard_map/rkpy,xqpyc->xqrkc/dot_general | solution.py:47
  150.6 6.4 %copy.131 = bf16[4,96,2,16,32]{4,3,2,0,1:T(8,128)(2,1)S(1)} copy(bf16[4,96,2,16,32]{1,3,2,4,0:T(8,128)(2,1)} %fusion.72) | data formatting | bytes 1572864 | tf_op jit(solution)/shard_map/convert_element_type | solution.py:52
  157.0 3.7 %reshape.528 = bf16[16,2,12288]{2,1,0:T(2,128)(2,1)} reshape(bf16[96,4,2,16,32]{4,3,2,1,0:T(8,128)(2,1)S(1)} %bitcast.284) | data formatting | bytes 1572864
  160.7 5.9 %all-to-all-start.2 = ((bf16[16,2,12288]{2,1,0:T(2,128)(2,1)}), bf16[16,2,12288]{2,1,0:T(2,128)(2,1)}, u32[]{:S(2)}, u32[]{:S(2)}) async-start(bf16[16,2,12288]{2,1,0:T(2,128)(2,1)} %reshape.528), calls=%async_computation.2 | async-start | bytes 1572864 | tf_op jit(solution)/shard_map/all_to_all | solution.py:53
  166.6 10.1 %all-gather = bf16[12,16,2,16,32]{4,3,2,1,0:T(8,128)(2,1)} all-gather(bf16[6,16,2,16,32]{4,3,2,1,0:T(8,128)(2,1)} %copy.147), channel_id=2, replica_groups=mesh['slab'=16,'dp'=2] {'dp'}, dimensions={0}, use_global_device_ids=true | all-gather | bytes 589824 | tf_op jit(solution)/shard_map/all_gather | solution.py:105
  176.7 14.5 %fusion.16 = f32[4,64,512,32]{2,3,1,0:T(8,128)} fusion(bf16[4,32,64,512]{3,2,1,0:T(8,128)(2,1)} %get-tuple-element.3, bf16[32,32]{1,0:T(8,128)(2,1)S(1)} %copy-done), kind=kOutput, calls=%fused_computation.27 | convolution fusion | flops 268435456 | bytes 25167872 | tf_op jit(solution)/shard_map/oc,xoyt->xcyt/dot_general | solution.py:47
  191.2 3.9 %reshape.529 = bf16[96,4,2,16,32]{4,3,2,1,0:T(8,128)(2,1)S(1)} reshape(bf16[16,2,12288]{2,1,0:T(2,128)(2,1)} %all-to-all-done.2) | data formatting | bytes 1572864
  195.1 0.9 copy.133
  196.0 2.0 fusion.81
  199.2 9.5 %fusion.77 = bf16[6,16,2,16,32,1]{4,2,3,1,0,5:T(2,128)(2,1)S(1)} fusion(bf16[6,16,16,32,64]{4,3,2,1,0:T(8,128)(2,1)} %param.7, bf16[6,16,2,16,64]{4,1,3,0,2:T(8,128)(2,1)S(1)} %pad_maximum_fusion), kind=kOutput, calls=%fused_computation.64 | convolution fusion | flops 12681216 | bytes 6881280 | tf_op jit(solution)/shard_map/qkyco,qkpyo->qkpyc/dot_general | solution.py:47
  208.8 1.8 fusion.66
  210.5 3.1 %all-gather.1 = bf16[12,16,2,16,32]{4,3,2,1,0:T(8,128)(2,1)} all-gather(bf16[6,16,2,16,32]{4,3,2,1,0:T(8,128)(2,1)S(1)} %copy.148), channel_id=3, replica_groups=mesh['slab'=16,'dp'=2] {'dp'}, dimensions={0}, use_global_device_ids=true | all-gather | bytes 589824 | tf_op jit(solution)/shard_map/all_gather | solution.py:106
  213.6 7.2 %copy.139 = bf16[64,6,2,16,32]{4,2,3,1,0:T(2,128)(2,1)S(1)} copy(bf16[64,6,2,16,32]{0,4,2,3,1:T(8,128)(2,1)} %fusion.66) | data formatting | bytes 1572864 | tf_op jit(solution)/shard_map/convert_element_type | solution.py:58
  220.8 3.7 %reshape.530 = bf16[16,2,12288]{2,1,0:T(2,128)(2,1)} reshape(bf16[64,6,16,2,32]{4,3,2,1,0:T(2,128)(2,1)S(1)} %bitcast.281) | data formatting | bytes 1572864
  224.6 7.2 %all-to-all-start.3 = ((bf16[16,2,12288]{2,1,0:T(2,128)(2,1)}), bf16[16,2,12288]{2,1,0:T(2,128)(2,1)}, u32[]{:S(2)}, u32[]{:S(2)}) async-start(bf16[16,2,12288]{2,1,0:T(2,128)(2,1)} %reshape.530), calls=%async_computation.3 | async-start | bytes 1572864 | tf_op jit(solution)/shard_map/all_to_all | solution.py:59
  231.8 1.6 fusion.126
  233.4 1.1 copy.256
  234.5 1.1 copy.257
  235.6 0.9 fusion.125
  236.5 4.3 %maximum_bitcast_fusion.1 = (bf16[2,6,16,1,16,64]{5,0,3,4,2,1:T(2,128)(2,1)S(1)}, bf16[2,6,16,1,16,64]{5,0,3,4,2,1:T(2,128)(2,1)S(1)}) fusion(bf16[2,6,16,16,32]{4,0,3,2,1:T(2,128)(2,1)S(1)} %bitcast.290, bf16[2,6,16,16,32]{4,0,3,2,1:T(2,128)(2,1)S(1)} %bitcast.291, bf16[2,6,16,16,32]{4,0,3,2,1:T(2,128)(2,1)S(1)} %fusion.125), kind=kLoop, calls=%fused_computation.73 | loop fusion | flops 1572864 | bytes 1376256 | tf_op jit(solution)/shard_map/stack | solution.py:69
  240.9 10.8 %convolution_bitcast_fusion = f32[6,16,16,32,64]{4,3,2,1,0:T(8,128)} fusion(bf16[2,6,16,1,16,64]{5,0,3,4,2,1:T(2,128)(2,1)S(1)} %get-tuple-element.10, bf16[2,6,16,1,16,64]{5,0,3,4,2,1:T(2,128)(2,1)S(1)} %get-tuple-element.9, bf16[2,6,16,2,16,32]{5,4,3,2,1,0:T(8,128)(2,1)S(1)} %bitcast.286), kind=kOutput, calls=%fused_computation.20 | convolution fusion | flops 26738688 | bytes 13762560 | tf_op jit(solution)/shard_map/sqkpyc,sqkpyo->qkyco/dot_general | solution.py:47
  251.9 7.2 %reshape.531 = bf16[64,6,16,2,32]{4,3,2,1,0:T(2,128)(2,1)S(1)} reshape(bf16[16,2,12288]{2,1,0:T(2,128)(2,1)} %all-to-all-done.3) | data formatting | bytes 1572864
  259.7 0.7 copy.141
  260.4 4.8 %copy.176 = bf16[4,96,2,16,32,1]{1,3,2,5,4,0:T(8,128)(2,1)} copy(bf16[4,96,2,16,32,1]{4,3,2,1,0,5:T(8,128)(2,1)S(1)} %bitcast.276) | data formatting | bytes 1572864 | tf_op jit(solution)/shard_map/all_to_all | solution.py:59
  265.2 21.6 %fusion.21 = bf16[1,4,32,64,512]{4,3,2,1,0:T(8,128)(2,1)} fusion(f32[4,64,512,32]{2,3,1,0:T(8,128)} %fusion.16, bf16[4,96,2,16,32,1]{1,3,2,5,4,0:T(8,128)(2,1)} %copy.176, bf16[1,96,512]{2,1,0:T(8,128)(2,1)S(1)} %get-tuple-element.16, bf16[1,96,512]{2,1,0:T(8,128)(2,1)S(1)} %get-tuple-element.15, bf16[1,16,2,64]{3,1,2,0:T(8,128)(2,1)S(1)} %get-tuple-element.18, ...), kind=kOutput, calls=%fused_computation.32 | convolution fusion | flops 1721634816 | bytes 26157056 | tf_op jit(solution)/shard_map/xqpyc,pqt->xcyt/dot_general | solution.py:47
  (23 shorter events, 2.1 us)
Async XLA Ops:
  0.6 84.1 %copy-start = (bf16[32,32]{1,0:T(8,128)(2,1)S(1)}, bf16[32,32]{1,0:T(8,128)(2,1)}, u32[]{:S(2)}) copy-start(bf16[32,32]{1,0:T(8,128)(2,1)} %param.8) | copy-start | bytes 6148
  55.1 10.1 %copy-start.2 = (bf16[6,16,2,16,32]{4,1,2,3,0:T(8,128)(2,1)}, bf16[6,16,2,16,32]{4,1,2,3,0:T(8,128)(2,1)S(1)}, u32[]{:S(2)}) copy-start(bf16[6,16,2,16,32]{4,1,2,3,0:T(8,128)(2,1)S(1)} %fusion.78) | copy-start | bytes 589828
  80.0 23.2 %all-to-all-start.1 = ((bf16[16,2,12288]{2,1,0:T(2,128)(2,1)}), bf16[16,2,12288]{2,1,0:T(2,128)(2,1)}, u32[]{:S(2)}, u32[]{:S(2)}) async-start(bf16[16,2,12288]{2,1,0:T(2,128)(2,1)} %reshape.526), calls=%async_computation.1 | async-start | bytes 1572864 | tf_op jit(solution)/shard_map/all_to_all | solution.py:59
  84.7 16.2 %copy-start.3 = (bf16[6,16,2,16,32]{4,1,2,3,0:T(8,128)(2,1)S(1)}, bf16[6,16,2,16,32]{4,1,2,3,0:T(8,128)(2,1)}, u32[]{:S(2)}) copy-start(bf16[6,16,2,16,32]{4,1,2,3,0:T(8,128)(2,1)} %copy-done.2) | copy-start | bytes 589828
  110.5 6.1 %copy-start.4 = (f32[32]{0:T(128)S(1)}, f32[32]{0:T(128)}, u32[]{:S(2)}) copy-start(f32[32]{0:T(128)} %param.9) | copy-start | bytes 388
  160.7 30.5 %all-to-all-start.2 = ((bf16[16,2,12288]{2,1,0:T(2,128)(2,1)}), bf16[16,2,12288]{2,1,0:T(2,128)(2,1)}, u32[]{:S(2)}, u32[]{:S(2)}) async-start(bf16[16,2,12288]{2,1,0:T(2,128)(2,1)} %reshape.528), calls=%async_computation.2 | async-start | bytes 1572864 | tf_op jit(solution)/shard_map/all_to_all | solution.py:53
  224.6 16.3 %copy-start.1 = (bf16[12,16,2,16,32]{4,3,2,1,0:T(8,128)(2,1)S(1)}, bf16[12,16,2,16,32]{4,3,2,1,0:T(8,128)(2,1)}, u32[]{:S(2)}) copy-start(bf16[12,16,2,16,32]{4,3,2,1,0:T(8,128)(2,1)} %all-gather) | copy-start | bytes 1179652
  224.6 27.4 %all-to-all-start.3 = ((bf16[16,2,12288]{2,1,0:T(2,128)(2,1)}), bf16[16,2,12288]{2,1,0:T(2,128)(2,1)}, u32[]{:S(2)}, u32[]{:S(2)}) async-start(bf16[16,2,12288]{2,1,0:T(2,128)(2,1)} %reshape.530), calls=%async_computation.3 | async-start | bytes 1572864 | tf_op jit(solution)/shard_map/all_to_all | solution.py:59
where the time goes:
time: 293 us; the launch traced here: 287 us
  matrix products  127 us (43%)
  local copies, waits for them, and re-layouts  83.9 us (29%)
  blocking collectives  43 us (15%)
  starting transfers between devices  17.8 us (6%)
  other arithmetic  12.6 us (4%)
    dot_general x13, matrix products, contract(): return jnp.einsum(form, left, right, preferred_element_type=jnp.float32)  127 us
    unnamed x20, local copies, waits for them, and re-layouts  39.4 us
    all_to_all x1, blocking collectives, analyse(): lax.all_to_all(second, 'slab', split_axis=1, concat_axis=0, tiled=True)  29.9 us
    convert_element_type x2, local copies, waits for them, and re-layouts, synthesise(): first = contract('pkrx,qkpyc->xqryc', outer, spectrum).astype(jnp.bfloat16)  14.5 us
    convert_element_type x2, local copies, waits for them, and re-layouts, analyse(): second = contract('rkpy,xqpyc->xqrkc', middle, first).astype(jnp.bfloat16)  12.8 us
    all_to_all x6, local copies, waits for them, and re-layouts, synthesise(): lax.all_to_all(first, 'slab', split_axis=0, concat_axis=1, tiled=True)  12.1 us
    all_to_all x2, starting transfers between devices, synthesise(): lax.all_to_all(first, 'slab', split_axis=0, concat_axis=1, tiled=True)  11.9 us
    all_gather x1, blocking collectives, per_device(): lax.all_gather(spectrum[None], 'dp', axis=0, tiled=True)  10.1 us
  transfers between devices with their start and end apart: 3, of which 2 were waited for; matrix products, arithmetic and copies ran while one was open for 18% of the time, Pallas kernels for 0%

commit v1 on v0

v1 whole, which is shorter than its diff:
```python
from functools import partial

import jax
import jax.numpy as jnp
import ml_dtypes
import numpy as np
from jax import lax
from jax.experimental import pallas as pl
from jax.experimental.pallas import tpu as pltpu
from jax.sharding import PartitionSpec as P

X = 64
Z = 32
T_SIZE = 16
MZ = 12
MT = 8
PARTS = 2
LIMIT = 52 * 1024 * 1024
BF = jnp.bfloat16
F32 = jnp.float32
NT = (((1,), (1,)), ((), ()))
TN = (((0,), (0,)), ((), ()))


def signed(m):
    i = np.arange(m)
    return np.where(i < m // 2, i, i - m)


def rounded(a):
    return np.asarray(a, np.float32).astype(ml_dtypes.bfloat16)


def waves(modes, length):
    angle = 2.0 * np.pi / length * ((signed(modes)[:, None] * np.arange(length)[None, :]) % length)
    return np.cos(angle), np.sin(angle)


def zt_waves():
    q = np.arange(MZ * MT)
    t = np.arange(Z * T_SIZE)
    total = Z * T_SIZE
    counts = (signed(MZ)[q // MT][:, None] * (t // T_SIZE)[None, :] * T_SIZE
              + (q % MT)[:, None] * (t % T_SIZE)[None, :] * Z) % total
    angle = 2.0 * np.pi / total * counts
    return np.cos(angle), -np.sin(angle)


class Tables:
    def __init__(self, n, xl, c, y, ql, mx, my, parts):
        xs = xl // parts
        i0, i1 = zt_waves()
        rows = np.arange(n * 2 * ql)
        dest, r, j = rows // (2 * ql), rows // ql % 2, rows % ql
        q = dest * ql + j
        first = np.where(r[:, None] == 0, i0[q], i1[q])
        second = np.where(r[:, None] == 0, i1[q], -i0[q])
        self.inner = rounded(np.concatenate([first, second], axis=1))
        cos, sin = waves(my, y)
        g = 4
        eye = np.eye(g)
        self.ya = rounded(np.stack([
            np.einsum("ab,ky->akby", eye, w).reshape(g * my, g * y) for w in (cos, sin)
        ]).reshape(2 * g * my, g * y))
        g = 8
        eye = np.eye(g)
        self.ys = rounded(np.concatenate([
            np.einsum("ab,ky->aybk", eye, w).reshape(g * y, g * my) for w in (cos, sin)
        ], axis=1))
        k = n * xs * 2 * ql
        out = np.arange(k)
        d, rest = out // (xs * 2 * ql), out % (xs * 2 * ql)
        x, w = rest // (2 * ql), rest % (2 * ql)
        src = (x * n + d) * 2 * ql + w
        perm = np.zeros((k, k))
        perm[out, src] = 1
        self.perm = rounded(perm)
        self.perm_t = rounded(perm.T)
        cx, sx = waves(mx, n * xl)
        big = np.zeros((2, 2, mx, n * xl))
        big[0, 0], big[0, 1], big[1, 0], big[1, 1] = cx, sx, -sx, cx
        full = np.einsum("rpkx,qj->qkrxpj", big, np.eye(ql))
        full = full.reshape(ql * mx * 2, n, parts, xs * 2 * ql)
        self.xa = rounded(full.transpose(2, 0, 1, 3).reshape(parts, ql * mx * 2, k))
        self.xs = rounded(full.transpose(2, 1, 3, 0).reshape(parts, k, ql * mx * 2))
        lanes = np.arange(c * my)
        swap = np.zeros((c * my, c * my))
        swap[lanes, lanes % my * c + lanes // my] = 1
        self.swap = rounded(swap)
        self.swap_t = rounded(swap.T)
        tile = np.zeros((c, c * my))
        tile[lanes // my, lanes] = 1
        self.tile = rounded(tile)
        spread = np.zeros((mx * 2 * my, mx * 2))
        spread[np.arange(mx * 2 * my), np.arange(mx * 2 * my) // my] = 1
        self.spread = rounded(spread)
        h = 16
        rep = np.zeros((c * h, c))
        rep[np.arange(c * h), np.arange(c * h) // h] = 1
        self.rep = rounded(rep)


def dot(a, b, dims=None):
    if dims is None:
        return jnp.dot(a, b, preferred_element_type=F32)
    return lax.dot_general(a, b, dims, preferred_element_type=F32)


def whole(a):
    return pl.BlockSpec(a.shape, lambda *_: (0,) * a.ndim)


def analyse_plane(load, ya, inner, v_ref, c, y, my):
    zt = inner.shape[1] // 2
    for g in range(c // 4):
        out = dot(ya[...], load(g).reshape(4 * y, zt)).astype(BF)
        v_ref[4 * my * g:4 * my * (g + 1), :zt] = out[:4 * my]
        v_ref[4 * my * g:4 * my * (g + 1), zt:] = out[4 * my:]
    return dot(inner[...], v_ref[...], NT).astype(BF)


def analyse_kernel(field, ya, inner, perm, out, v_ref, all_ref):
    i, steps = pl.program_id(0), pl.num_programs(0)
    c, y = field.shape[2:4]
    my = v_ref.shape[0] // c
    rows = inner.shape[0]
    spec = analyse_plane(lambda g: field[0, 0, 4 * g:4 * g + 4], ya, inner, v_ref, c, y, my)
    all_ref[pl.ds(pl.multiple_of(i * rows, rows), rows), :] = spec

    @pl.when(i == steps - 1)
    def _():
        out[...] = dot(perm[...], all_ref[...]).astype(BF)


def params():
    return pltpu.CompilerParams(vmem_limit_bytes=LIMIT)


def analyse(field, tab, part, xs, my):
    _, _, c, y, zt = field.shape
    rows = tab.inner.shape[0]
    args = [jnp.asarray(tab.ya), jnp.asarray(tab.inner), jnp.asarray(tab.perm)]
    return pl.pallas_call(
        analyse_kernel,
        grid=(xs,),
        in_specs=[pl.BlockSpec((1, 1, c, y, zt), lambda i: (0, part * xs + i, 0, 0, 0))] + [whole(a) for a in args],
        out_specs=pl.BlockSpec((xs * rows, c * my), lambda i: (0, 0)),
        out_shape=jax.ShapeDtypeStruct((xs * rows, c * my), BF),
        scratch_shapes=[pltpu.VMEM((c * my, 2 * zt), BF), pltpu.VMEM((xs * rows, c * my), BF)],
        compiler_params=params(),
        name="analyse",
    )(field, *args)


def row_mask(rows, lanes, my, by_minor, c):
    row = lax.broadcasted_iota(jnp.int32, (rows, lanes), 0) % my
    lane = lax.broadcasted_iota(jnp.int32, (rows, lanes), 1)
    return row == (lane % my if by_minor else lane // c)


def mix_kernel(parts, my, scale, *refs):
    recv = refs[:parts]
    w, xa, xs, swap, tile, spread = refs[parts:parts + 6]
    outs = refs[parts + 6:2 * parts + 6]
    spec_out, spec, mixed, both = refs[2 * parts + 6:]
    i, steps = pl.program_id(0), pl.num_programs(0)
    c, mx = w.shape[3], w.shape[1]
    lanes = c * my

    @pl.when(i == 0)
    def _():
        total = dot(xa[0], recv[0][...])
        for p in range(1, parts):
            total += dot(xa[p], recv[p][...])
        spec[...] = dot(total.astype(BF), swap[...]).astype(BF)
        spec_out[...] = spec[...]

    here = pl.ds(pl.multiple_of(i * mx * 2, mx * 2), mx * 2)
    rep = dot(spread[...], spec[here, :])
    block = jnp.where(row_mask(mx * 2 * my, lanes, my, False, c), rep, 0.0).astype(BF)
    for k in range(mx):
        both[2 * my * k:2 * my * (k + 1), :] = dot(
            block[2 * my * k:2 * my * (k + 1)], w[0, k].reshape(lanes, 2 * c))
    b = both[...].reshape(mx, 2, my, 2 * c)
    b0, b1 = b[:, 0], b[:, 1]
    real = b0[..., :c] - b1[..., c:]
    imag = b0[..., c:] + b1[..., :c]
    small = jnp.stack([real, imag], axis=1).reshape(mx * 2 * my, c).astype(BF)
    wide = dot(small, tile[...])
    wide = jnp.where(row_mask(mx * 2 * my, lanes, my, True, c), wide, 0.0).astype(BF)
    mixed[here, :] = dot(spread[...], wide, TN).astype(BF)

    @pl.when(i == steps - 1)
    def _():
        for p in range(parts):
            outs[p][...] = (dot(xs[p], mixed[...]) * scale).astype(BF)


def mix(recv, weight, tab, my, scale):
    parts = len(recv)
    ql, mx, _, c, _ = weight.shape
    lanes = c * my
    args = [jnp.asarray(a) for a in (tab.xa, tab.xs, tab.swap, tab.tile, tab.spread)]
    rows = ql * mx * 2
    out_shape = [jax.ShapeDtypeStruct(r.shape, BF) for r in recv] + [jax.ShapeDtypeStruct((rows, lanes), BF)]
    return pl.pallas_call(
        partial(mix_kernel, parts, my, scale),
        grid=(ql,),
        in_specs=[whole(r) for r in recv]
        + [pl.BlockSpec((1, mx, my, c, 2 * c), lambda i: (i, 0, 0, 0, 0))]
        + [whole(a) for a in args],
        out_specs=[whole(a) for a in out_shape],
        out_shape=out_shape,
        scratch_shapes=[pltpu.VMEM((rows, lanes), BF), pltpu.VMEM((rows, lanes), BF),
                        pltpu.VMEM((mx * 2 * my, 2 * c), F32)],
        compiler_params=params(),
        name="mix",
    )(*recv, weight, *args)


def pair_rows(g, tile, spread, mask, mx, my, c):
    rep = jnp.where(mask, dot(spread[...], g), 0.0).astype(BF)
    small = dot(rep, tile[...], NT).reshape(mx, 2, my, c)
    real, imag = small[:, 0], small[:, 1]
    first = jnp.concatenate([real, imag], axis=-1)
    second = jnp.concatenate([imag, -real], axis=-1)
    return jnp.stack([first, second], axis=1).reshape(mx * 2 * my, 2 * c).astype(BF)


def back_kernel(parts, my, scale, *refs):
    recv = refs[:parts]
    w, xa, xs, swap_t, tile, spread = refs[parts:parts + 6]
    outs = refs[parts + 6:2 * parts + 6]
    spec_out, spec, mixed, wide = refs[2 * parts + 6:]
    i, steps = pl.program_id(0), pl.num_programs(0)
    c, mx = w.shape[3], w.shape[1]
    lanes = c * my

    @pl.when(i == 0)
    def _():
        total = dot(xa[0], recv[0][...])
        for p in range(1, parts):
            total += dot(xa[p], recv[p][...])
        spec[...] = (total * scale).astype(BF)
        spec_out[...] = spec[...]

    here = pl.ds(pl.multiple_of(i * mx * 2, mx * 2), mx * 2)
    mask = row_mask(mx * 2 * my, lanes, my, True, c)
    pair = pair_rows(spec[here, :], tile, spread, mask, mx, my, c)
    block = row_mask(2 * my, lanes, my, False, c)
    for k in range(mx):
        out = dot(pair[2 * my * k:2 * my * (k + 1)], w[0, k].reshape(lanes, 2 * c), NT)
        wide[2 * my * k:2 * my * (k + 1), :] = jnp.where(block, out, 0.0).astype(BF)
    mixed[here, :] = dot(spread[...], wide[...], TN).astype(BF)

    @pl.when(i == steps - 1)
    def _():
        turned = dot(mixed[...], swap_t[...]).astype(BF)
        for p in range(parts):
            outs[p][...] = dot(xs[p], turned).astype(BF)


def back(recv, weight, tab, my, scale):
    parts = len(recv)
    ql, mx, _, c, _ = weight.shape
    lanes = c * my
    args = [jnp.asarray(a) for a in (tab.xa, tab.xs, tab.swap_t, tab.tile, tab.spread)]
    rows = ql * mx * 2
    out_shape = [jax.ShapeDtypeStruct(r.shape, BF) for r in recv] + [jax.ShapeDtypeStruct((rows, lanes), BF)]
    return pl.pallas_call(
        partial(back_kernel, parts, my, scale),
        grid=(ql,),
        in_specs=[whole(r) for r in recv]
        + [pl.BlockSpec((1, mx, my, c, 2 * c), lambda i: (i, 0, 0, 0, 0))]
        + [whole(a) for a in args],
        out_specs=[whole(a) for a in out_shape],
        out_shape=out_shape,
        scratch_shapes=[pltpu.VMEM((rows, lanes), BF), pltpu.VMEM((rows, lanes), BF),
                        pltpu.VMEM((mx * 2 * my, lanes), BF)],
        compiler_params=params(),
        name="back",
    )(*recv, weight, *args)


def weight_kernel(samples, my, *refs):
    specs, grads = refs[:samples], refs[samples:2 * samples]
    tile, spread, out = refs[2 * samples:]
    mx, c = out.shape[1], out.shape[3]
    lanes = c * my
    rows = mx * 2 * my
    minor = row_mask(rows, lanes, my, True, c)
    major = row_mask(rows, lanes, my, False, c)
    blocks, pairs = [], []
    for s in range(samples):
        blocks.append(jnp.where(major, dot(spread[...], specs[s][...]), 0.0).astype(BF))
        pairs.append(pair_rows(grads[s][...], tile, spread, minor, mx, my, c))
    for k in range(mx):
        cut = slice(2 * my * k, 2 * my * (k + 1))
        left = jnp.concatenate([b[cut] for b in blocks], axis=0)
        right = jnp.concatenate([b[cut] for b in pairs], axis=0)
        out[0, k] = dot(left, right, TN).reshape(my, c, 2 * c)


def weight_gradient(specs, grads, shape, tab):
    ql, mx, my, c, _ = shape
    lanes = c * my
    args = [jnp.asarray(tab.tile), jnp.asarray(tab.spread)]
    block = pl.BlockSpec((mx * 2, lanes), lambda i: (i, 0))
    return pl.pallas_call(
        partial(weight_kernel, len(specs), my),
        grid=(ql,),
        in_specs=[block] * (2 * len(specs)) + [whole(a) for a in args],
        out_specs=pl.BlockSpec((1, mx, my, c, 2 * c), lambda i: (i, 0, 0, 0, 0)),
        out_shape=jax.ShapeDtypeStruct(shape, F32),
        compiler_params=params(),
        name="weight_gradient",
    )(*specs, *grads, *args)


def expand_point(point, rep, kron, transposed):
    half = dot(rep[...], point[...], (((1,), (0 if not transposed else 1,)), ((), ()))).astype(BF)
    full = dot(half, rep[...], NT)
    n = full.shape[0]
    row = lax.broadcasted_iota(jnp.int32, (n, n), 0) % 16
    lane = lax.broadcasted_iota(jnp.int32, (n, n), 1) % 16
    kron[...] = jnp.where(row == lane, full, 0.0).astype(BF)


def linear_plane(load, kron, acc, c, y):
    for j in range(y // 16):
        block = load(j)
        zt = block.shape[-1]
        acc[:, 16 * j:16 * j + 16, :] = dot(kron[...], block.reshape(c * 16, zt)).reshape(c, 16, zt)


def synth_group(g, v, ys, my, zt):
    rows = 8 * my
    cut = slice(rows * g, rows * (g + 1))
    both = jnp.concatenate([v[cut, :zt], v[cut, zt:]], axis=0)
    return dot(ys[...], both)


def forward_kernel(aliased, field, cot, recv, ys, ya, inner, perm, perm_t, rep, point, bias, *refs):
    if aliased:
        refs = refs[1:]
    layer, grad, out, all_in, all_out, v_ref, kron, acc = refs
    i, steps = pl.program_id(0), pl.num_programs(0)
    c, y, zt = field.shape[2:]
    my = v_ref.shape[0] // c
    rows = inner.shape[0]

    @pl.when(i == 0)
    def _():
        all_in[...] = dot(perm_t[...], recv[...]).astype(BF)
        expand_point(point, rep, kron, False)

    here = pl.ds(pl.multiple_of(i * rows, rows), rows)
    v_ref[...] = dot(all_in[here, :], inner[...], TN).astype(BF)
    linear_plane(lambda j: field[0, 0, :, 16 * j:16 * j + 16, :], kron, acc, c, y)
    k0 = float(np.sqrt(2.0 / np.pi))
    k1 = k0 * 0.044715
    for g in range(c // 8):
        spectral = synth_group(g, v_ref, ys, my, zt)
        for h in range(8):
            ch = 8 * g + h
            pre = spectral[y * h:y * (h + 1)] + (acc[ch] + bias[ch])
            sq = pre * pre
            th = jnp.tanh(pre * (k0 + k1 * sq))
            cdf = 0.5 + 0.5 * th
            layer[0, 0, ch] = (pre * cdf).astype(BF)
            slope = cdf + (0.5 * pre) * ((1.0 - th * th) * (k0 + (3.0 * k1) * sq))
            grad[0, ch] = (cot[0, 0, ch].astype(F32) * slope).astype(BF)
    all_out[here, :] = analyse_plane(lambda g: grad[0, 4 * g:4 * g + 4], ya, inner, v_ref, c, y, my)

    @pl.when(i == steps - 1)
    def _():
        out[...] = dot(perm[...], all_out[...]).astype(BF)


def forward(field, cot, recv, point, bias, earlier, tab, part, xs, my):
    _, _, c, y, zt = field.shape
    rows = tab.inner.shape[0]
    args = [recv] + [jnp.asarray(a) for a in (tab.ys, tab.ya, tab.inner, tab.perm, tab.perm_t, tab.rep)] + [point]
    plane = pl.BlockSpec((1, 1, c, y, zt), lambda i: (0, part * xs + i, 0, 0, 0))
    specs = [plane, plane] + [whole(a) for a in args] + [pl.BlockSpec(memory_space=pltpu.SMEM)]
    operands = [field, cot, *args, bias]
    aliases = {}
    if earlier is not None:
        aliases = {len(operands): 0}
        operands.append(earlier)
        specs.append(pl.BlockSpec(memory_space=pl.ANY))
    return pl.pallas_call(
        partial(forward_kernel, earlier is not None),
        grid=(xs,),
        in_specs=specs,
        out_specs=[plane, pl.BlockSpec((1, c, y, zt), lambda i: (i, 0, 0, 0)), whole(recv)],
        out_shape=[jax.ShapeDtypeStruct(field.shape, BF), jax.ShapeDtypeStruct((xs, c, y, zt), BF),
                   jax.ShapeDtypeStruct(recv.shape, BF)],
        scratch_shapes=[pltpu.VMEM((xs * rows, c * my), BF), pltpu.VMEM((xs * rows, c * my), BF),
                        pltpu.VMEM((c * my, 2 * zt), BF), pltpu.VMEM((c * 16, c * 16), BF),
                        pltpu.VMEM((c, y, zt), F32)],
        input_output_aliases=aliases,
        compiler_params=params(),
        name="forward",
    )(*operands)


def final_kernel(aliased, grad, recv, ys, inner, perm_t, rep, point, *refs):
    if aliased:
        refs = refs[1:]
    out, all_in, v_ref, kron, acc = refs
    i = pl.program_id(0)
    c, y, zt = grad.shape[1:]
    my = v_ref.shape[0] // c
    rows = inner.shape[0]

    @pl.when(i == 0)
    def _():
        all_in[...] = dot(perm_t[...], recv[...]).astype(BF)
        expand_point(point, rep, kron, True)

    here = pl.ds(pl.multiple_of(i * rows, rows), rows)
    v_ref[...] = dot(all_in[here, :], inner[...], TN).astype(BF)
    linear_plane(lambda j: grad[0, :, 16 * j:16 * j + 16, :], kron, acc, c, y)
    for g in range(c // 8):
        spectral = synth_group(g, v_ref, ys, my, zt).reshape(8, y, zt)
        out[0, 0, 8 * g:8 * g + 8] = (spectral + acc[8 * g:8 * g + 8]).astype(BF)


def final(grad, recv, point, earlier, shape, tab, part, my):
    xs, c, y, zt = grad.shape
    rows = tab.inner.shape[0]
    args = [recv] + [jnp.asarray(a) for a in (tab.ys, tab.inner, tab.perm_t, tab.rep)] + [point]
    specs = [pl.BlockSpec((1, c, y, zt), lambda i: (i, 0, 0, 0))] + [whole(a) for a in args]
    operands = [grad, *args]
    aliases = {}
    if earlier is not None:
        aliases = {len(operands): 0}
        operands.append(earlier)
        specs.append(pl.BlockSpec(memory_space=pl.ANY))
    return pl.pallas_call(
        partial(final_kernel, earlier is not None),
        grid=(xs,),
        in_specs=specs,
        out_specs=pl.BlockSpec((1, 1, c, y, zt), lambda i: (0, part * xs + i, 0, 0, 0)),
        out_shape=jax.ShapeDtypeStruct(shape, BF),
        scratch_shapes=[pltpu.VMEM((xs * rows, c * my), BF), pltpu.VMEM((c * my, 2 * zt), BF),
                        pltpu.VMEM((c * 16, c * 16), BF), pltpu.VMEM((c, y, zt), F32)],
        input_output_aliases=aliases,
        compiler_params=params(),
        name="final",
    )(*operands)


def exchange(block, n):
    shape = block.shape
    block = block.reshape(n, shape[0] // n, shape[1])
    block = lax.all_to_all(block, "slab", split_axis=0, concat_axis=0, tiled=True)
    return block.reshape(shape)


def samples_of(a, dp):
    return [a] + [
        lax.ppermute(a, "dp", [(j, (j + s) % dp) for j in range(dp)]) for s in range(1, dp)
    ]


def per_device(n, dp, field, cotangent, spectral_weight, point_weight, bias_term):
    _, xl, c, y, zt = field.shape
    ql, mx, my = spectral_weight.shape[:3]
    parts = PARTS if xl % PARTS == 0 else 1
    xs = xl // parts
    tab = Tables(n, xl, c, y, ql, mx, my, parts)
    scale = 1.0 / (n * xl * y * zt)
    recv = [exchange(analyse(field, tab, p, xs, my), n) for p in range(parts)]
    *sent, spec = mix(recv, spectral_weight, tab, my, scale)
    specs = samples_of(spec, dp)
    recv = [exchange(a, n) for a in sent]
    layer, grads, sent = None, [], []
    for p in range(parts):
        layer, grad, out = forward(field, cotangent, recv[p], point_weight, bias_term, layer, tab, p, xs, my)
        grads.append(grad)
        sent.append(exchange(out, n))
    *sent, gspec = back(sent, spectral_weight, tab, my, scale)
    gspecs = samples_of(gspec, dp)
    recv = [exchange(a, n) for a in sent]
    weight_grad = weight_gradient(specs, gspecs, spectral_weight.shape, tab)
    total = None
    for p in range(parts):
        total = final(grads[p], recv[p], point_weight, total, field.shape, tab, p, my)
    return layer, total, weight_grad


def solution(mesh):
    spread = P("dp", "slab", None, None, None)
    modes = P("slab", None, None, None, None)
    return jax.shard_map(
        partial(per_device, mesh.shape["slab"], mesh.shape["dp"]),
        mesh=mesh,
        in_specs=(spread, spread, modes, P(), P()),
        out_specs=(spread, spread, modes),
        check_vma=False,
    )
```

time: 293 us -> 192 us (0.66); the launches traced: 287 us -> 191 us
  matrix products: 127 us -> 0 us
  Pallas kernels: 0 us -> 91.9 us
  local copies, waits for them, and re-layouts: 83.9 us -> 2.85 us
  blocking collectives: 43 us -> 62.1 us
  other arithmetic: 12.6 us -> 0 us
  waiting for transfers between devices: 1.35 us -> 10.1 us
  starting transfers between devices: 17.8 us -> 23.2 us
    dot_general x13 -> x0, matrix products: 127 us -> none  [contract(): return jnp.einsum(form, left, right, preferred_element_type=jnp.float32)]
    pallas_call x0 -> x9, Pallas kernels: none -> 91.9 us  [the longest x2 30.8 us: forward(): pl.pallas_call(partial(forward_kernel, earlier is not None), grid=(xs,),...]
    unnamed x20 -> x30, local copies, waits for them, and re-layouts: 39.4 us -> 2.85 us
    all_to_all x1 -> x4, blocking collectives: 29.9 us -> 62.1 us  [exchange(): lax.all_to_all(block, 'slab', split_axis=0, concat_axis=0, tiled=True)]
    convert_element_type x6 -> x0, local copies, waits for them, and re-layouts: 28.7 us -> none  [the longest x2 14.5 us: synthesise(): first = contract('pkrx,qkpyc->xqryc', outer, spectrum).astype(jnp.bfloat16)]
    all_to_all x8 -> x0, local copies, waits for them, and re-layouts: 13.9 us -> none  [the longest x6 12.1 us: synthesise(): lax.all_to_all(first, 'slab', split_axis=0, concat_axis=1, tiled=True)]
    all_gather x2 -> x0, blocking collectives: 13.1 us -> none  [the longest x1 10.1 us: per_device(): lax.all_gather(spectrum[None], 'dp', axis=0, tiled=True)]
    another operation x8 -> x0, other arithmetic: 11.6 us -> none  [the longest x3 4.92 us: pairs(): return jnp.stack([first, second], axis=-3)]
  transfers between devices with their start and end apart: 3 -> 6, of which waited for: 2 -> 3; matrix products, arithmetic and copies ran while one was open for 18% -> 0% of each run, Pallas kernels for 0% -> 29%
where the time goes in v1:
time: 192 us; the launch traced here: 191 us
  Pallas kernels  91.9 us (48%)
  blocking collectives  62.1 us (32%)
  starting transfers between devices  23.2 us (12%)
  waiting for transfers between devices  10.1 us (5%)
  local copies, waits for them, and re-layouts  2.85 us (1%)
    all_to_all x4, blocking collectives, exchange(): lax.all_to_all(block, 'slab', split_axis=0, concat_axis=0, tiled=True)  62.1 us
    pallas_call x2, Pallas kernels, forward(): pl.pallas_call(partial(forward_kernel, earlier is not None), grid=(xs,),...  30.8 us
    all_to_all x4, starting transfers between devices, exchange(): lax.all_to_all(block, 'slab', split_axis=0, concat_axis=0, tiled=True)  22.7 us
    pallas_call x2, Pallas kernels, final(): pl.pallas_call(partial(final_kernel, earlier is not None), grid=(xs,), in...  15.5 us
    pallas_call x1, Pallas kernels, weight_gradient(): pl.pallas_call(partial(weight_kernel, len(specs), my), grid=(ql,), in_spe...  13.6 us
    pallas_call x1, Pallas kernels, back(): pl.pallas_call(partial(back_kernel, parts, my, scale), grid=(ql,), in_spe...  12.9 us
    pallas_call x1, Pallas kernels, mix(): pl.pallas_call(partial(mix_kernel, parts, my, scale), grid=(ql,), in_spec...  10.9 us
    all_to_all x4, waiting for transfers between devices, exchange(): lax.all_to_all(block, 'slab', split_axis=0, concat_axis=0, tiled=True)  8.93 us
  transfers between devices with their start and end apart: 6, of which 3 were waited for; matrix products, arithmetic and copies ran while one was open for 0% of the time, Pallas kernels for 29%

profile of v1, /device:TPU:0, one launch (start us, length us, event | category | flops | bytes accessed | tf_op | source)
XLA Modules:
  0.0 191.1 jit_solution(12889138226960137829)
XLA Ops:
  0.6 0.0 copy-start
  0.6 1.0 copy-done
  1.6 0.0 copy-start.4
  1.6 1.0 copy-done.4
  2.6 0.0 copy-start.9
  2.6 0.8 copy-done.9
  3.4 0.0 copy-start.1
  3.4 0.0 copy-start.8
  3.5 0.0 copy-start.11
  3.5 4.5 %analyse.3 = bf16[384,512]{1,0:T(8,128)(2,1)} custom-call(bf16[1,4,32,64,512]{4,3,2,1,0:T(8,128)(2,1)} %field.7, bf16[128,256]{1,0:T(8,128)(2,1)S(1)} %copy-done.9, bf16[192,1024]{1,0:T(8,128)(2,1)S(1)} %copy-done, bf16[384,384]{1,0:T(8,128)(2,1)S(1)} %copy-done.4), custom_call_target="tpu_custom_call" | custom-call | tf_op jit(solution)/shard_map/analyse/pallas_call | solution.py:143
  8.0 8.3 %all-to-all-start.1 = ((bf16[16,24,512]{2,1,0:T(8,128)(2,1)}), bf16[16,24,512]{2,1,0:T(8,128)(2,1)S(1)}, u32[]{:S(2)}, u32[]{:S(2)}) async-start(bf16[16,24,512]{2,1,0:T(8,128)(2,1)} %bitcast.2), calls=%async_computation.1 | async-start | bytes 786432 | tf_op jit(solution)/shard_map/all_to_all | solution.py:458
  16.3 0.0 copy-done.1
  16.3 0.0 copy-done.5
  16.3 0.0 copy-done.10
  16.3 3.7 %analyse.2 = bf16[384,512]{1,0:T(8,128)(2,1)S(1)} custom-call(bf16[1,4,32,64,512]{4,3,2,1,0:T(8,128)(2,1)} %field.7, bf16[128,256]{1,0:T(8,128)(2,1)S(1)} %copy-done.10, bf16[192,1024]{1,0:T(8,128)(2,1)S(1)} %copy-done.1, bf16[384,384]{1,0:T(8,128)(2,1)S(1)} %copy-done.5), custom_call_target="tpu_custom_call" | custom-call | tf_op jit(solution)/shard_map/analyse/pallas_call | solution.py:143
  20.0 8.9 %all-to-all-done.1 = bf16[16,24,512]{2,1,0:T(8,128)(2,1)S(1)} async-done(((bf16[16,24,512]{2,1,0:T(8,128)(2,1)}), bf16[16,24,512]{2,1,0:T(8,128)(2,1)S(1)}, u32[]{:S(2)}, u32[]{:S(2)}) %all-to-all-start.1) | async-done | bytes 393248 | tf_op jit(solution)/shard_map/all_to_all | solution.py:458
  29.0 0.0 copy-start.13
  29.0 15.5 %all_to_all.40 = bf16[16,24,512]{2,1,0:T(8,128)(2,1)S(1)} all-to-all(bf16[16,24,512]{2,1,0:T(8,128)(2,1)S(1)} %bitcast.17), channel_id=1, replica_groups=mesh['slab'=16,'dp'=2] {'slab'}, dimensions={0} | all-to-all | bytes 786432 | tf_op jit(solution)/shard_map/all_to_all | solution.py:458
  44.5 0.0 copy-done.14
  44.5 0.0 copy-done.3
  44.5 0.0 copy-done.8
  44.5 0.0 copy-done.11
  44.5 10.9 %mix.1 = (bf16[384,512]{1,0:T(8,128)(2,1)S(1)}, bf16[384,512]{1,0:T(8,128)(2,1)}, bf16[192,512]{1,0:T(8,128)(2,1)S(1)}) custom-call(bf16[384,512]{1,0:T(8,128)(2,1)S(1)} %bitcast.22, bf16[384,512]{1,0:T(8,128)(2,1)} %bitcast.26, bf16[6,16,16,32,64]{4,3,2,1,0:T(8,128)(2,1)} %refs_2_.3, bf16[2,192,384]{2,1,0:T(8,128)(2,1)S(1)} %copy-done.8, ...), custom_call_target="tpu_custom_call" | custom-call | tf_op jit(solution)/shard_map/mix/pallas_call | solution.py:206
  55.4 15.0 %all_to_all.41 = bf16[16,24,512]{2,1,0:T(8,128)(2,1)S(1)} all-to-all(bf16[16,24,512]{2,1,0:T(8,128)(2,1)S(1)} %bitcast.25), channel_id=1, replica_groups=mesh['slab'=16,'dp'=2] {'slab'}, dimensions={0} | all-to-all | bytes 786432 | tf_op jit(solution)/shard_map/all_to_all | solution.py:458
  70.4 3.6 %all-to-all-start.2 = ((bf16[16,24,512]{2,1,0:T(8,128)(2,1)}), bf16[16,24,512]{2,1,0:T(8,128)(2,1)S(1)}, u32[]{:S(2)}, u32[]{:S(2)}) async-start(bf16[16,24,512]{2,1,0:T(8,128)(2,1)} %bitcast.4), calls=%async_computation.2 | async-start | bytes 786432 | tf_op jit(solution)/shard_map/all_to_all | solution.py:458
  74.0 0.0 copy-done.6
  74.0 0.0 copy-done.7
  74.0 0.0 copy-done.12
  74.1 0.0 copy-done.13
  74.1 15.5 %forward.2 = (bf16[1,4,32,64,512]{4,3,2,1,0:T(8,128)(2,1)}, bf16[2,32,64,512]{3,2,1,0:T(8,128)(2,1)}, bf16[384,512]{1,0:T(8,128)(2,1)}) custom-call(bf16[1,4,32,64,512]{4,3,2,1,0:T(8,128)(2,1)} %field.7, bf16[1,4,32,64,512]{4,3,2,1,0:T(8,128)(2,1)} %cot.3, bf16[384,512]{1,0:T(8,128)(2,1)S(1)} %bitcast.21, bf16[512,256]{1,0:T(8,128)(2,1)S(1)} %copy-done.7, ...), custom_call_target="tpu_custom_call" | custom-call | tf_op jit(solution)/shard_map/forward/pallas_call | solution.py:392
  89.5 0.0 all-to-all-done.2
  89.5 6.9 %all-to-all-start.4 = ((bf16[16,24,512]{2,1,0:T(8,128)(2,1)}), bf16[16,24,512]{2,1,0:T(8,128)(2,1)S(1)}, u32[]{:S(2)}, u32[]{:S(2)}) async-start(bf16[16,24,512]{2,1,0:T(8,128)(2,1)} %bitcast.8), calls=%async_computation.4 | async-start | bytes 786432 | tf_op jit(solution)/shard_map/all_to_all | solution.py:458
  96.5 15.3 %forward.3 = (bf16[1,4,32,64,512]{4,3,2,1,0:T(8,128)(2,1)}, bf16[2,32,64,512]{3,2,1,0:T(8,128)(2,1)}, bf16[384,512]{1,0:T(8,128)(2,1)S(1)}) custom-call(bf16[1,4,32,64,512]{4,3,2,1,0:T(8,128)(2,1)} %field.7, bf16[1,4,32,64,512]{4,3,2,1,0:T(8,128)(2,1)} %cot.3, bf16[384,512]{1,0:T(8,128)(2,1)S(1)} %bitcast.20, ...), custom_call_target="tpu_custom_call", output_to_operand_aliasing={{0}: (11, {})} | custom-call | tf_op jit(solution)/shard_map/forward/pallas_call | solution.py:392
  111.8 0.0 all-to-all-done.4
  111.8 16.9 %all_to_all.42 = bf16[16,24,512]{2,1,0:T(8,128)(2,1)} all-to-all(bf16[16,24,512]{2,1,0:T(8,128)(2,1)S(1)} %bitcast.23), channel_id=1, replica_groups=mesh['slab'=16,'dp'=2] {'slab'}, dimensions={0} | all-to-all | bytes 786432 | tf_op jit(solution)/shard_map/all_to_all | solution.py:458
  128.7 12.9 %back.1 = (bf16[384,512]{1,0:T(8,128)(2,1)S(1)}, bf16[384,512]{1,0:T(8,128)(2,1)}, bf16[192,512]{1,0:T(8,128)(2,1)S(1)}) custom-call(bf16[384,512]{1,0:T(8,128)(2,1)S(1)} %bitcast.19, bf16[384,512]{1,0:T(8,128)(2,1)} %bitcast.27, bf16[6,16,16,32,64]{4,3,2,1,0:T(8,128)(2,1)} %refs_2_.3, bf16[2,192,384]{2,1,0:T(8,128)(2,1)S(1)} %copy-done.8, ...), custom_call_target="tpu_custom_call" | custom-call | tf_op jit(solution)/shard_map/back/pallas_call | solution.py:270
  141.6 14.7 %all_to_all.43 = bf16[16,24,512]{2,1,0:T(8,128)(2,1)S(1)} all-to-all(bf16[16,24,512]{2,1,0:T(8,128)(2,1)S(1)} %bitcast.24), channel_id=1, replica_groups=mesh['slab'=16,'dp'=2] {'slab'}, dimensions={0} | all-to-all | bytes 786432 | tf_op jit(solution)/shard_map/all_to_all | solution.py:458
  156.4 3.8 %all-to-all-start.6 = ((bf16[16,24,512]{2,1,0:T(8,128)(2,1)}), bf16[16,24,512]{2,1,0:T(8,128)(2,1)S(1)}, u32[]{:S(2)}, u32[]{:S(2)}) async-start(bf16[16,24,512]{2,1,0:T(8,128)(2,1)} %bitcast.12), calls=%async_computation.6 | async-start | bytes 786432 | tf_op jit(solution)/shard_map/all_to_all | solution.py:458
  160.2 0.1 collective-permute-start
  160.3 0.0 copy-start.2
  160.3 0.5 collective-permute-start.1
  160.8 0.9 collective-permute-done.refs_1_
  161.7 0.3 collective-permute-done.1.refs_3_
  162.0 13.6 %weight_gradient.1 = f32[6,16,16,32,64]{4,3,2,1,0:T(8,128)} custom-call(bf16[192,512]{1,0:T(8,128)(2,1)S(1)} %get-tuple-element.25.refs_0_, bf16[192,512]{1,0:T(8,128)(2,1)S(1)} %collective-permute-done.refs_1_, bf16[192,512]{1,0:T(8,128)(2,1)S(1)} %get-tuple-element.26.refs_2_, bf16[192,512]{1,0:T(8,128)(2,1)S(1)} %collective-permute-done.1.refs_3_, ...), custom_call_target="tpu_custom_call" | custom-call | tf_op jit(solution)/shard_map/weight_gradient/pallas_call | solution.py:309
  175.6 0.0 copy-done.2
  175.6 7.7 %final.2.refs_0_ = bf16[1,4,32,64,512]{4,3,2,1,0:T(8,128)(2,1)} custom-call(bf16[2,32,64,512]{3,2,1,0:T(8,128)(2,1)} %get-tuple-element.23.grad, bf16[384,512]{1,0:T(8,128)(2,1)S(1)} %bitcast.16, bf16[512,256]{1,0:T(8,128)(2,1)S(1)} %copy-done.7, bf16[192,1024]{1,0:T(8,128)(2,1)S(1)} %copy-done.2, bf16[384,384]{1,0:T(8,128)(2,1)S(1)} %copy-done.6, ...), custom_call_target="tpu_custom_call" | custom-call | tf_op jit(solution)/shard_map/final/pallas_call | solution.py:441
  183.3 0.0 all-to-all-done.6
  183.3 7.8 %final.3 = bf16[1,4,32,64,512]{4,3,2,1,0:T(8,128)(2,1)} custom-call(bf16[2,32,64,512]{3,2,1,0:T(8,128)(2,1)} %get-tuple-element.19.grad, bf16[384,512]{1,0:T(8,128)(2,1)S(1)} %bitcast.18, bf16[512,256]{1,0:T(8,128)(2,1)S(1)} %copy-done.7, bf16[192,1024]{1,0:T(8,128)(2,1)S(1)} %copy-done.2, ...), custom_call_target="tpu_custom_call", output_to_operand_aliasing={{}: (7, {})} | custom-call | tf_op jit(solution)/shard_map/final/pallas_call | solution.py:441
  (7 shorter events, 0.0 us)
Async XLA Ops:
  0.6 1.0 copy-start
  1.6 1.0 copy-start.4
  2.6 0.8 copy-start.9
  3.4 12.9 %copy-start.1 = (bf16[192,1024]{1,0:T(8,128)(2,1)S(1)}, bf16[192,1024]{1,0:T(8,128)(2,1)}, u32[]{:S(2)}) copy-start(bf16[192,1024]{1,0:T(8,128)(2,1)} %constant.23.clone.inner) | copy-start | bytes 1179652
  3.4 12.9 %copy-start.5 = (bf16[384,384]{1,0:T(8,128)(2,1)S(1)}, bf16[384,384]{1,0:T(8,128)(2,1)}, u32[]{:S(2)}) copy-start(bf16[384,384]{1,0:T(8,128)(2,1)} %constant.24.clone.perm) | copy-start | bytes 884740
  3.4 12.9 %copy-start.10 = (bf16[128,256]{1,0:T(8,128)(2,1)S(1)}, bf16[128,256]{1,0:T(8,128)(2,1)}, u32[]{:S(2)}) copy-start(bf16[128,256]{1,0:T(8,128)(2,1)} %constant.22.clone.ya) | copy-start | bytes 196612
  3.4 41.0 %copy-start.3 = (bf16[512,32]{1,0:T(8,128)(2,1)S(1)}, bf16[512,32]{1,0:T(8,128)(2,1)}, u32[]{:S(2)}) copy-start(bf16[512,32]{1,0:T(8,128)(2,1)} %constant.29.clone.refs_7_.rep.refs_5_) | copy-start | bytes 98308
  3.4 41.0 %copy-start.8 = (bf16[2,192,384]{2,1,0:T(8,128)(2,1)S(1)}, bf16[2,192,384]{2,1,0:T(8,128)(2,1)}, u32[]{:S(2)}) copy-start(bf16[2,192,384]{2,1,0:T(8,128)(2,1)} %constant.25.clone.refs_3_) | copy-start | bytes 884740
  3.5 41.0 %copy-start.11 = (bf16[32,512]{1,0:T(8,128)(2,1)S(1)}, bf16[32,512]{1,0:T(8,128)(2,1)}, u32[]{:S(2)}) copy-start(bf16[32,512]{1,0:T(8,128)(2,1)} %constant.28.clone.refs_6_.refs_4_) | copy-start | bytes 98308
  8.0 21.0 %all-to-all-start.1 = ((bf16[16,24,512]{2,1,0:T(8,128)(2,1)}), bf16[16,24,512]{2,1,0:T(8,128)(2,1)S(1)}, u32[]{:S(2)}, u32[]{:S(2)}) async-start(bf16[16,24,512]{2,1,0:T(8,128)(2,1)} %bitcast.2), calls=%async_computation.1 | async-start | bytes 786432 | tf_op jit(solution)/shard_map/all_to_all | solution.py:458
  28.9 15.5 %copy-start.14 = (bf16[16,24,512]{2,1,0:T(8,128)(2,1)}, bf16[16,24,512]{2,1,0:T(8,128)(2,1)S(1)}, u32[]{:S(2)}) copy-start(bf16[16,24,512]{2,1,0:T(8,128)(2,1)S(1)} %all-to-all-done.1) | copy-start | bytes 1179652
  28.9 45.1 %copy-start.6 = (bf16[384,384]{1,0:T(8,128)(2,1)S(1)}, bf16[384,384]{1,0:T(8,128)(2,1)}, u32[]{:S(2)}) copy-start(bf16[384,384]{1,0:T(8,128)(2,1)} %constant.31.clone.perm_t) | copy-start | bytes 884740
  28.9 45.1 %copy-start.7 = (bf16[512,256]{1,0:T(8,128)(2,1)S(1)}, bf16[512,256]{1,0:T(8,128)(2,1)}, u32[]{:S(2)}) copy-start(bf16[512,256]{1,0:T(8,128)(2,1)} %constant.30.clone.ys) | copy-start | bytes 786436
  29.0 45.1 %copy-start.12 = (bf16[32,32]{1,0:T(8,128)(2,1)S(1)}, bf16[32,32]{1,0:T(8,128)(2,1)}, u32[]{:S(2)}) copy-start(bf16[32,32]{1,0:T(8,128)(2,1)} %point.7) | copy-start | bytes 6148
  29.0 45.1 %copy-start.13 = (f32[32]{0:T(128)S(1)}, f32[32]{0:T(128)}, u32[]{:S(2)}) copy-start(f32[32]{0:T(128)} %bias.3) | copy-start | bytes 388
  70.4 19.1 %all-to-all-start.2 = ((bf16[16,24,512]{2,1,0:T(8,128)(2,1)}), bf16[16,24,512]{2,1,0:T(8,128)(2,1)S(1)}, u32[]{:S(2)}, u32[]{:S(2)}) async-start(bf16[16,24,512]{2,1,0:T(8,128)(2,1)} %bitcast.4), calls=%async_computation.2 | async-start | bytes 786432 | tf_op jit(solution)/shard_map/all_to_all | solution.py:458
  89.5 22.3 %all-to-all-start.4 = ((bf16[16,24,512]{2,1,0:T(8,128)(2,1)}), bf16[16,24,512]{2,1,0:T(8,128)(2,1)S(1)}, u32[]{:S(2)}, u32[]{:S(2)}) async-start(bf16[16,24,512]{2,1,0:T(8,128)(2,1)} %bitcast.8), calls=%async_computation.4 | async-start | bytes 786432 | tf_op jit(solution)/shard_map/all_to_all | solution.py:458
  156.4 26.9 %all-to-all-start.6 = ((bf16[16,24,512]{2,1,0:T(8,128)(2,1)}), bf16[16,24,512]{2,1,0:T(8,128)(2,1)S(1)}, u32[]{:S(2)}, u32[]{:S(2)}) async-start(bf16[16,24,512]{2,1,0:T(8,128)(2,1)} %bitcast.12), calls=%async_computation.6 | async-start | bytes 786432 | tf_op jit(solution)/shard_map/all_to_all | solution.py:458
  160.2 1.5 collective-permute-start
  160.3 15.3 %copy-start.2 = (bf16[192,1024]{1,0:T(8,128)(2,1)S(1)}, bf16[192,1024]{1,0:T(8,128)(2,1)}, u32[]{:S(2)}) copy-start(bf16[192,1024]{1,0:T(8,128)(2,1)} %constant.23.clone.inner) | copy-start | bytes 1179652
  160.3 1.7 collective-permute-start.1

commit v2 on v1

--- a/solution.py
+++ b/solution.py
@@ -14,7 +14,7 @@
 T_SIZE = 16
 MZ = 12
 MT = 8
-PARTS = 2
+PARTS = 1
 LIMIT = 52 * 1024 * 1024
 BF = jnp.bfloat16
 F32 = jnp.float32
@@ -452,6 +452,42 @@
     )(*operands)
 
 
+def swap_kernel(n, src, dst, send, recv, own):
+    me = lax.axis_index("slab")
+    barrier = pltpu.get_barrier_semaphore()
+    for k in range(1, n):
+        pl.semaphore_signal(barrier, inc=1, device_id={"slab": lax.rem(me + k, n)},
+                            device_id_type=pl.DeviceIdType.MESH)
+    local = pltpu.make_async_copy(src.at[me], dst.at[me], own)
+    local.start()
+    pl.semaphore_wait(barrier, n - 1)
+    copies = []
+    for k in range(1, n):
+        to = lax.rem(me + k, n)
+        copies.append(pltpu.make_async_remote_copy(
+            src_ref=src.at[to], dst_ref=dst.at[me], send_sem=send.at[k], recv_sem=recv.at[k],
+            device_id={"slab": to}, device_id_type=pl.DeviceIdType.MESH))
+        copies[-1].start()
+    local.wait()
+    for copy in copies:
+        copy.wait()
+
+
+def push(block, n):
+    shape = block.shape
+    block = block.reshape(n, shape[0] // n, shape[1])
+    out = pl.pallas_call(
+        partial(swap_kernel, n),
+        in_specs=[pl.BlockSpec(memory_space=pltpu.VMEM)],
+        out_specs=pl.BlockSpec(memory_space=pltpu.VMEM),
+        out_shape=jax.ShapeDtypeStruct(block.shape, BF),
+        scratch_shapes=[pltpu.SemaphoreType.DMA((n,)), pltpu.SemaphoreType.DMA((n,)), pltpu.SemaphoreType.DMA],
+        compiler_params=pltpu.CompilerParams(collective_id=0, has_side_effects=True, vmem_limit_bytes=16 * 1024 * 1024),
+        name="push",
+    )(block)
+    return out.reshape(shape)
+
+
 def exchange(block, n):
     shape = block.shape
     block = block.reshape(n, shape[0] // n, shape[1])
@@ -472,15 +508,15 @@
     xs = xl // parts
     tab = Tables(n, xl, c, y, ql, mx, my, parts)
     scale = 1.0 / (n * xl * y * zt)
-    recv = [exchange(analyse(field, tab, p, xs, my), n) for p in range(parts)]
+    recv = [push(analyse(field, tab, p, xs, my), n) for p in range(parts)]
     *sent, spec = mix(recv, spectral_weight, tab, my, scale)
     specs = samples_of(spec, dp)
-    recv = [exchange(a, n) for a in sent]
+    recv = [push(a, n) for a in sent]
     layer, grads, sent = None, [], []
     for p in range(parts):
         layer, grad, out = forward(field, cotangent, recv[p], point_weight, bias_term, layer, tab, p, xs, my)
         grads.append(grad)
-        sent.append(exchange(out, n))
+        sent.append(push(out, n))
     *sent, gspec = back(sent, spectral_weight, tab, my, scale)
     gspecs = samples_of(gspec, dp)
     recv = [exchange(a, n) for a in sent]

time: 192 us -> 169 us (0.88)
  blocking collectives: 62.1 us -> 0 us
  Pallas kernels: 91.9 us -> 146 us
  starting transfers between devices: 23.2 us -> 11.3 us
  waiting for transfers between devices: 10.1 us -> 4.2 us
  local copies, waits for them, and re-layouts: 2.85 us -> 5.63 us
    all_to_all x4 -> x0, blocking collectives: 62.1 us -> none  [exchange(): lax.all_to_all(block, 'slab', split_axis=0, concat_axis=0, tiled=True)]
    pallas_call x0 -> x3, Pallas kernels: none -> 61.2 us  [push(): pl.pallas_call(partial(swap_kernel, n), in_specs=[pl.BlockSpec(memory_spa...]
    all_to_all x4 -> x1, starting transfers between devices: 22.7 us -> 10.7 us  [exchange(): lax.all_to_all(block, 'slab', split_axis=0, concat_axis=0, tiled=True)]
    all_to_all x4 -> x1, waiting for transfers between devices: 8.93 us -> 2.99 us  [exchange(): lax.all_to_all(block, 'slab', split_axis=0, concat_axis=0, tiled=True)]
    pallas_call x2 -> x1, Pallas kernels: 30.8 us -> 27.3 us  [forward(): pl.pallas_call(partial(forward_kernel, earlier is not None), grid=(xs,),...]
    unnamed x30 -> x32, local copies, waits for them, and re-layouts: 2.85 us -> 5.63 us
    pallas_call x2 -> x1, Pallas kernels: 15.5 us -> 13 us  [final(): pl.pallas_call(partial(final_kernel, earlier is not None), grid=(xs,), in...]
    pallas_call x2 -> x1, Pallas kernels: 8.2 us -> 7.11 us  [analyse(): pl.pallas_call(analyse_kernel, grid=(xs,), in_specs=[pl.BlockSpec((1, 1,...]
  transfers between devices with their start and end apart: 6 -> 3, of which waited for: 3 -> 3; matrix products, arithmetic and copies ran while one was open for 0% -> 0% of each run, Pallas kernels for 29% -> 8%
where the time goes in v2:
time: 169 us; the launch traced here: 168 us
  Pallas kernels  146 us (86%)
  starting transfers between devices  11.3 us (7%)
  local copies, waits for them, and re-layouts  5.63 us (3%)
  waiting for transfers between devices  4.2 us (2%)
    pallas_call x3, Pallas kernels, push(): pl.pallas_call(partial(swap_kernel, n), in_specs=[pl.BlockSpec(memory_spa...  61.2 us
    pallas_call x1, Pallas kernels, forward(): pl.pallas_call(partial(forward_kernel, earlier is not None), grid=(xs,),...  27.3 us
    pallas_call x1, Pallas kernels, weight_gradient(): pl.pallas_call(partial(weight_kernel, len(specs), my), grid=(ql,), in_spe...  13.6 us
    pallas_call x1, Pallas kernels, final(): pl.pallas_call(partial(final_kernel, earlier is not None), grid=(xs,), in...  13 us
    pallas_call x1, Pallas kernels, back(): pl.pallas_call(partial(back_kernel, parts, my, scale), grid=(ql,), in_spe...  12.9 us
    pallas_call x1, Pallas kernels, mix(): pl.pallas_call(partial(mix_kernel, parts, my, scale), grid=(ql,), in_spec...  10.9 us
    all_to_all x1, starting transfers between devices, exchange(): lax.all_to_all(block, 'slab', split_axis=0, concat_axis=0, tiled=True)  10.7 us
    pallas_call x1, Pallas kernels, analyse(): pl.pallas_call(analyse_kernel, grid=(xs,), in_specs=[pl.BlockSpec((1, 1,...  7.11 us
  transfers between devices with their start and end apart: 3, of which 3 were waited for; matrix products, arithmetic and copies ran while one was open for 0% of the time, Pallas kernels for 8%

profile of v2, /device:TPU:0, one launch (start us, length us, event | category | flops | bytes accessed | tf_op | source)
XLA Modules:
  0.0 167.9 jit_solution(13527688899547421568)
XLA Ops:
  0.6 0.0 copy-start
  0.6 1.0 copy-done
  1.6 0.0 copy-start.13
  1.6 0.8 copy-done.13
  2.5 0.0 copy-start.2
  2.5 0.0 copy-start.6
  2.5 0.0 copy-start.7
  2.5 0.0 copy-start.11
  2.5 0.0 copy-start.12
  2.5 7.1 %analyse.1 = bf16[768,512]{1,0:T(8,128)(2,1)S(1)} custom-call(bf16[1,4,32,64,512]{4,3,2,1,0:T(8,128)(2,1)} %field.3, bf16[128,256]{1,0:T(8,128)(2,1)S(1)} %copy-done.13, bf16[192,1024]{1,0:T(8,128)(2,1)S(1)} %copy-done, bf16[768,768]{1,0:T(8,128)(2,1)} %constant.24.clone.perm), custom_call_target="tpu_custom_call" | custom-call | tf_op jit(solution)/shard_map/analyse/pallas_call | solution.py:143
  9.6 19.9 %push.3 = bf16[16,48,512]{2,1,0:T(8,128)(2,1)S(1)} custom-call(bf16[16,48,512]{2,1,0:T(8,128)(2,1)S(1)} %bitcast.12), custom_call_target="tpu_custom_call" | custom-call | tf_op jit(solution)/shard_map/push/pallas_call | solution.py:479
  29.5 0.0 copy-start.5
  29.5 0.9 copy-done.5
  30.4 0.0 copy-start.1
  30.4 0.0 copy-start.8
  30.4 0.0 copy-start.14
  30.4 0.0 copy-start.15
  30.4 0.0 copy-done.2
  30.4 0.0 copy-done.6
  30.4 0.0 copy-done.7
  30.4 0.0 copy-done.11
  30.4 0.0 copy-done.12
  30.4 10.9 %mix.1 = (bf16[768,512]{1,0:T(8,128)(2,1)}, bf16[192,512]{1,0:T(8,128)(2,1)S(1)}) custom-call(bf16[768,512]{1,0:T(8,128)(2,1)} %bitcast.11, bf16[6,16,16,32,64]{4,3,2,1,0:T(8,128)(2,1)} %refs_1_.3, bf16[1,192,768]{2,1,0:T(8,128)(2,1)S(1)} %copy-done.7, bf16[1,768,192]{2,1,0:T(8,128)(2,1)S(1)} %copy-done.6, bf16[512,512]{1,0:T(8,128)(2,1)S(1)} %copy-done.11, ...), custom_call_target="tpu_custom_call" | custom-call | tf_op jit(solution)/shard_map/mix/pallas_call | solution.py:206
  41.3 0.0 copy-start.9
  41.3 1.1 copy-done.9
  42.5 21.2 %push.4 = bf16[16,48,512]{2,1,0:T(8,128)(2,1)S(1)} custom-call(bf16[16,48,512]{2,1,0:T(8,128)(2,1)S(1)} %bitcast.14), custom_call_target="tpu_custom_call" | custom-call | tf_op jit(solution)/shard_map/push/pallas_call | solution.py:479
  63.7 0.0 copy-start.3
  63.7 0.9 copy-done.3
  64.6 0.0 copy-done.1
  64.6 0.0 copy-done.8
  64.6 0.0 copy-done.14
  64.6 0.0 copy-done.15
  64.6 0.0 copy-start.10
  64.6 27.3 %forward.1 = (bf16[1,4,32,64,512]{4,3,2,1,0:T(8,128)(2,1)}, bf16[4,32,64,512]{3,2,1,0:T(8,128)(2,1)}, bf16[768,512]{1,0:T(8,128)(2,1)S(1)}) custom-call(bf16[1,4,32,64,512]{4,3,2,1,0:T(8,128)(2,1)} %field.3, bf16[1,4,32,64,512]{4,3,2,1,0:T(8,128)(2,1)} %cot.1, bf16[768,512]{1,0:T(8,128)(2,1)} %bitcast.9, bf16[512,256]{1,0:T(8,128)(2,1)S(1)} %copy-done.8, ...), custom_call_target="tpu_custom_call" | custom-call | tf_op jit(solution)/shard_map/forward/pallas_call | solution.py:392
  91.9 20.1 %push.5 = bf16[16,48,512]{2,1,0:T(8,128)(2,1)S(1)} custom-call(bf16[16,48,512]{2,1,0:T(8,128)(2,1)S(1)} %bitcast.13), custom_call_target="tpu_custom_call" | custom-call | tf_op jit(solution)/shard_map/push/pallas_call | solution.py:479
  112.0 0.0 copy-start.4
  112.0 0.9 copy-done.4
  112.9 0.0 copy-done.10
  112.9 12.9 %back.1 = (bf16[768,512]{1,0:T(8,128)(2,1)}, bf16[192,512]{1,0:T(8,128)(2,1)S(1)}) custom-call(bf16[768,512]{1,0:T(8,128)(2,1)} %bitcast.10, bf16[6,16,16,32,64]{4,3,2,1,0:T(8,128)(2,1)} %refs_1_.3, bf16[1,192,768]{2,1,0:T(8,128)(2,1)S(1)} %copy-done.7, bf16[1,768,192]{2,1,0:T(8,128)(2,1)S(1)} %copy-done.6, bf16[512,512]{1,0:T(8,128)(2,1)S(1)} %copy-done.10, ...), custom_call_target="tpu_custom_call" | custom-call | tf_op jit(solution)/shard_map/back/pallas_call | solution.py:270
  125.7 10.7 %all-to-all-start = ((bf16[16,48,512]{2,1,0:T(8,128)(2,1)}), bf16[16,48,512]{2,1,0:T(8,128)(2,1)S(1)}, u32[]{:S(2)}, u32[]{:S(2)}) async-start(bf16[16,48,512]{2,1,0:T(8,128)(2,1)} %bitcast.15), calls=%async_computation | async-start | bytes 1572864 | tf_op jit(solution)/shard_map/all_to_all | solution.py:494
  136.5 0.1 collective-permute-start
  136.6 0.5 collective-permute-start.1
  137.1 0.9 collective-permute-done.refs_1_
  138.0 0.3 collective-permute-done.1.refs_3_
  138.3 13.6 %weight_gradient.1 = f32[6,16,16,32,64]{4,3,2,1,0:T(8,128)} custom-call(bf16[192,512]{1,0:T(8,128)(2,1)S(1)} %get-tuple-element.15.refs_0_, bf16[192,512]{1,0:T(8,128)(2,1)S(1)} %collective-permute-done.refs_1_, bf16[192,512]{1,0:T(8,128)(2,1)S(1)} %get-tuple-element.16.refs_2_, bf16[192,512]{1,0:T(8,128)(2,1)S(1)} %collective-permute-done.1.refs_3_, ...), custom_call_target="tpu_custom_call" | custom-call | tf_op jit(solution)/shard_map/weight_gradient/pallas_call | solution.py:309
  151.9 3.0 %all-to-all-done = bf16[16,48,512]{2,1,0:T(8,128)(2,1)S(1)} async-done(((bf16[16,48,512]{2,1,0:T(8,128)(2,1)}), bf16[16,48,512]{2,1,0:T(8,128)(2,1)S(1)}, u32[]{:S(2)}, u32[]{:S(2)}) %all-to-all-start) | async-done | bytes 786464 | tf_op jit(solution)/shard_map/all_to_all | solution.py:494
  154.9 13.0 %final.1 = bf16[1,4,32,64,512]{4,3,2,1,0:T(8,128)(2,1)} custom-call(bf16[4,32,64,512]{3,2,1,0:T(8,128)(2,1)} %get-tuple-element.12.grad, bf16[768,512]{1,0:T(8,128)(2,1)S(1)} %bitcast.8, bf16[512,256]{1,0:T(8,128)(2,1)S(1)} %copy-done.8, bf16[192,1024]{1,0:T(8,128)(2,1)S(1)} %copy-done.1, bf16[768,768]{1,0:T(8,128)(2,1)} %constant.31.clone.perm_t, ...), custom_call_target="tpu_custom_call" | custom-call | tf_op jit(solution)/shard_map/final/pallas_call | solution.py:441
Async XLA Ops:
  0.6 1.0 copy-start
  1.6 0.8 copy-start.13
  2.5 27.9 %copy-start.2 = (bf16[512,32]{1,0:T(8,128)(2,1)S(1)}, bf16[512,32]{1,0:T(8,128)(2,1)}, u32[]{:S(2)}) copy-start(bf16[512,32]{1,0:T(8,128)(2,1)} %constant.29.clone.refs_6_.rep.refs_5_) | copy-start | bytes 98308
  2.5 27.9 %copy-start.6 = (bf16[1,768,192]{2,1,0:T(8,128)(2,1)S(1)}, bf16[1,768,192]{2,1,0:T(8,128)(2,1)}, u32[]{:S(2)}) copy-start(bf16[1,768,192]{2,1,0:T(8,128)(2,1)} %constant.26.clone.refs_3_) | copy-start | bytes 884740
  2.5 27.9 %copy-start.7 = (bf16[1,192,768]{2,1,0:T(8,128)(2,1)S(1)}, bf16[1,192,768]{2,1,0:T(8,128)(2,1)}, u32[]{:S(2)}) copy-start(bf16[1,192,768]{2,1,0:T(8,128)(2,1)} %constant.25.clone.refs_2_) | copy-start | bytes 884740
  2.5 28.0 %copy-start.11 = (bf16[512,512]{1,0:T(8,128)(2,1)S(1)}, bf16[512,512]{1,0:T(8,128)(2,1)}, u32[]{:S(2)}) copy-start(bf16[512,512]{1,0:T(8,128)(2,1)} %constant.27.clone.refs_4_) | copy-start | bytes 1572868
  2.5 28.0 %copy-start.12 = (bf16[32,512]{1,0:T(8,128)(2,1)S(1)}, bf16[32,512]{1,0:T(8,128)(2,1)}, u32[]{:S(2)}) copy-start(bf16[32,512]{1,0:T(8,128)(2,1)} %constant.28.clone.refs_5_.refs_4_) | copy-start | bytes 98308
  29.5 0.9 copy-start.5
  30.4 34.2 %copy-start.1 = (bf16[192,1024]{1,0:T(8,128)(2,1)S(1)}, bf16[192,1024]{1,0:T(8,128)(2,1)}, u32[]{:S(2)}) copy-start(bf16[192,1024]{1,0:T(8,128)(2,1)} %constant.23.clone.inner) | copy-start | bytes 1179652
  30.4 34.2 %copy-start.8 = (bf16[512,256]{1,0:T(8,128)(2,1)S(1)}, bf16[512,256]{1,0:T(8,128)(2,1)}, u32[]{:S(2)}) copy-start(bf16[512,256]{1,0:T(8,128)(2,1)} %constant.30.clone.ys) | copy-start | bytes 786436
  30.4 34.2 %copy-start.14 = (bf16[32,32]{1,0:T(8,128)(2,1)S(1)}, bf16[32,32]{1,0:T(8,128)(2,1)}, u32[]{:S(2)}) copy-start(bf16[32,32]{1,0:T(8,128)(2,1)} %point.3) | copy-start | bytes 6148
  30.4 34.2 %copy-start.15 = (f32[32]{0:T(128)S(1)}, f32[32]{0:T(128)}, u32[]{:S(2)}) copy-start(f32[32]{0:T(128)} %bias.1) | copy-start | bytes 388
  41.3 1.1 copy-start.9
  63.7 0.9 copy-start.3
  64.6 48.2 %copy-start.10 = (bf16[512,512]{1,0:T(8,128)(2,1)S(1)}, bf16[512,512]{1,0:T(8,128)(2,1)}, u32[]{:S(2)}) copy-start(bf16[512,512]{1,0:T(8,128)(2,1)} %constant.32.clone.refs_4_) | copy-start | bytes 1572868
  112.0 0.9 copy-start.4
  125.7 29.2 %all-to-all-start = ((bf16[16,48,512]{2,1,0:T(8,128)(2,1)}), bf16[16,48,512]{2,1,0:T(8,128)(2,1)S(1)}, u32[]{:S(2)}, u32[]{:S(2)}) async-start(bf16[16,48,512]{2,1,0:T(8,128)(2,1)} %bitcast.15), calls=%async_computation | async-start | bytes 1572864 | tf_op jit(solution)/shard_map/all_to_all | solution.py:494
  136.5 1.5 collective-permute-start
  136.6 1.7 %collective-permute-start.1 = (bf16[192,512]{1,0:T(8,128)(2,1)S(1)}, bf16[192,512]{1,0:T(8,128)(2,1)S(1)}, u32[]{:S(2)}, u32[]{:S(2)}) collective-permute-start(bf16[192,512]{1,0:T(8,128)(2,1)S(1)} %get-tuple-element.16.refs_2_), channel_id=1, source_target_pairs={{0,1},{1,0},{2,3},{3,2},{4,5},{5,4},{6,7},{7,6},{8,9},{9,8},{10,11... | collective-permute-start | bytes 589832 | tf_op jit(solution)/shard_map/ppermute | solution.py:500

commit v3 on v2

--- a/solution.py
+++ b/solution.py
@@ -462,7 +462,7 @@
     local.start()
     pl.semaphore_wait(barrier, n - 1)
     copies = []
-    for k in range(1, n):
+    for k in sorted(range(1, n), key=lambda k: abs(2 * k - n)):
         to = lax.rem(me + k, n)
         copies.append(pltpu.make_async_remote_copy(
             src_ref=src.at[to], dst_ref=dst.at[me], send_sem=send.at[k], recv_sem=recv.at[k],

time: 169 us -> 168 us (level)
  starting transfers between devices: 11.3 us -> 5.8 us
  Pallas kernels: 146 us -> 151 us
    all_to_all x1, starting transfers between devices: 10.7 us -> 5.23 us  [exchange(): lax.all_to_all(block, 'slab', split_axis=0, concat_axis=0, tiled=True)]
    pallas_call x3, Pallas kernels: 61.2 us -> 66.4 us  [push(): pl.pallas_call(partial(swap_kernel, n), in_specs=[pl.BlockSpec(memory_spa...]
where the time goes in v3:
time: 168 us
  Pallas kernels  151 us (90%)
  starting transfers between devices  5.8 us (3%)
  local copies, waits for them, and re-layouts  5.63 us (3%)
  waiting for transfers between devices  4.34 us (3%)
    pallas_call x3, Pallas kernels, push(): pl.pallas_call(partial(swap_kernel, n), in_specs=[pl.BlockSpec(memory_spa...  66.4 us
    pallas_call x1, Pallas kernels, forward(): pl.pallas_call(partial(forward_kernel, earlier is not None), grid=(xs,),...  27.3 us
    pallas_call x1, Pallas kernels, weight_gradient(): pl.pallas_call(partial(weight_kernel, len(specs), my), grid=(ql,), in_spe...  13.6 us
    pallas_call x1, Pallas kernels, final(): pl.pallas_call(partial(final_kernel, earlier is not None), grid=(xs,), in...  13 us
    pallas_call x1, Pallas kernels, back(): pl.pallas_call(partial(back_kernel, parts, my, scale), grid=(ql,), in_spe...  12.9 us
    pallas_call x1, Pallas kernels, mix(): pl.pallas_call(partial(mix_kernel, parts, my, scale), grid=(ql,), in_spec...  10.9 us
    pallas_call x1, Pallas kernels, analyse(): pl.pallas_call(analyse_kernel, grid=(xs,), in_specs=[pl.BlockSpec((1, 1,...  7.11 us
    unnamed x32, local copies, waits for them, and re-layouts  5.63 us
  transfers between devices with their start and end apart: 3, of which 3 were waited for; matrix products, arithmetic and copies ran while one was open for 0% of the time, Pallas kernels for 8%

profile of v3, /device:TPU:0, one launch (start us, length us, event | category | flops | bytes accessed | tf_op | source)
XLA Modules:
  0.0 167.7 jit_solution(17336105244183529300)
XLA Ops:
  0.6 0.0 copy-start
  0.6 1.0 copy-done
  1.6 0.0 copy-start.13
  1.6 0.8 copy-done.13
  2.5 0.0 copy-start.2
  2.5 0.0 copy-start.6
  2.5 0.0 copy-start.7
  2.5 0.0 copy-start.11
  2.5 0.0 copy-start.12
  2.5 7.1 %analyse.1 = bf16[768,512]{1,0:T(8,128)(2,1)S(1)} custom-call(bf16[1,4,32,64,512]{4,3,2,1,0:T(8,128)(2,1)} %field.3, bf16[128,256]{1,0:T(8,128)(2,1)S(1)} %copy-done.13, bf16[192,1024]{1,0:T(8,128)(2,1)S(1)} %copy-done, bf16[768,768]{1,0:T(8,128)(2,1)} %constant.24.clone.perm), custom_call_target="tpu_custom_call" | custom-call | tf_op jit(solution)/shard_map/analyse/pallas_call | solution.py:143
  9.6 23.1 %push.3 = bf16[16,48,512]{2,1,0:T(8,128)(2,1)S(1)} custom-call(bf16[16,48,512]{2,1,0:T(8,128)(2,1)S(1)} %bitcast.12), custom_call_target="tpu_custom_call" | custom-call | tf_op jit(solution)/shard_map/push/pallas_call | solution.py:479
  32.7 0.0 copy-start.5
  32.7 0.9 copy-done.5
  33.6 0.0 copy-start.1
  33.6 0.0 copy-start.8
  33.6 0.0 copy-start.14
  33.6 0.0 copy-start.15
  33.6 0.0 copy-done.2
  33.6 0.0 copy-done.6
  33.6 0.0 copy-done.7
  33.6 0.0 copy-done.11
  33.7 0.0 copy-done.12
  33.7 10.9 %mix.1 = (bf16[768,512]{1,0:T(8,128)(2,1)}, bf16[192,512]{1,0:T(8,128)(2,1)S(1)}) custom-call(bf16[768,512]{1,0:T(8,128)(2,1)} %bitcast.11, bf16[6,16,16,32,64]{4,3,2,1,0:T(8,128)(2,1)} %refs_1_.3, bf16[1,192,768]{2,1,0:T(8,128)(2,1)S(1)} %copy-done.7, bf16[1,768,192]{2,1,0:T(8,128)(2,1)S(1)} %copy-done.6, bf16[512,512]{1,0:T(8,128)(2,1)S(1)} %copy-done.11, ...), custom_call_target="tpu_custom_call" | custom-call | tf_op jit(solution)/shard_map/mix/pallas_call | solution.py:206
  44.6 0.0 copy-start.9
  44.6 1.1 copy-done.9
  45.7 22.6 %push.4 = bf16[16,48,512]{2,1,0:T(8,128)(2,1)S(1)} custom-call(bf16[16,48,512]{2,1,0:T(8,128)(2,1)S(1)} %bitcast.14), custom_call_target="tpu_custom_call" | custom-call | tf_op jit(solution)/shard_map/push/pallas_call | solution.py:479
  68.3 0.0 copy-start.3
  68.3 0.9 copy-done.3
  69.2 0.0 copy-done.1
  69.2 0.0 copy-done.8
  69.2 0.0 copy-done.14
  69.2 0.0 copy-done.15
  69.2 0.0 copy-start.10
  69.2 27.3 %forward.1 = (bf16[1,4,32,64,512]{4,3,2,1,0:T(8,128)(2,1)}, bf16[4,32,64,512]{3,2,1,0:T(8,128)(2,1)}, bf16[768,512]{1,0:T(8,128)(2,1)S(1)}) custom-call(bf16[1,4,32,64,512]{4,3,2,1,0:T(8,128)(2,1)} %field.3, bf16[1,4,32,64,512]{4,3,2,1,0:T(8,128)(2,1)} %cot.1, bf16[768,512]{1,0:T(8,128)(2,1)} %bitcast.9, bf16[512,256]{1,0:T(8,128)(2,1)S(1)} %copy-done.8, ...), custom_call_target="tpu_custom_call" | custom-call | tf_op jit(solution)/shard_map/forward/pallas_call | solution.py:392
  96.5 20.6 %push.5 = bf16[16,48,512]{2,1,0:T(8,128)(2,1)S(1)} custom-call(bf16[16,48,512]{2,1,0:T(8,128)(2,1)S(1)} %bitcast.13), custom_call_target="tpu_custom_call" | custom-call | tf_op jit(solution)/shard_map/push/pallas_call | solution.py:479
  117.1 0.0 copy-start.4
  117.2 0.9 copy-done.4
  118.0 0.0 copy-done.10
  118.0 12.9 %back.1 = (bf16[768,512]{1,0:T(8,128)(2,1)}, bf16[192,512]{1,0:T(8,128)(2,1)S(1)}) custom-call(bf16[768,512]{1,0:T(8,128)(2,1)} %bitcast.10, bf16[6,16,16,32,64]{4,3,2,1,0:T(8,128)(2,1)} %refs_1_.3, bf16[1,192,768]{2,1,0:T(8,128)(2,1)S(1)} %copy-done.7, bf16[1,768,192]{2,1,0:T(8,128)(2,1)S(1)} %copy-done.6, bf16[512,512]{1,0:T(8,128)(2,1)S(1)} %copy-done.10, ...), custom_call_target="tpu_custom_call" | custom-call | tf_op jit(solution)/shard_map/back/pallas_call | solution.py:270
  130.9 5.2 %all-to-all-start = ((bf16[16,48,512]{2,1,0:T(8,128)(2,1)}), bf16[16,48,512]{2,1,0:T(8,128)(2,1)S(1)}, u32[]{:S(2)}, u32[]{:S(2)}) async-start(bf16[16,48,512]{2,1,0:T(8,128)(2,1)} %bitcast.15), calls=%async_computation | async-start | bytes 1572864 | tf_op jit(solution)/shard_map/all_to_all | solution.py:494
  136.2 0.1 collective-permute-start
  136.2 0.5 collective-permute-start.1
  136.7 0.9 collective-permute-done.refs_1_
  137.7 0.3 collective-permute-done.1.refs_3_
  137.9 13.6 %weight_gradient.1 = f32[6,16,16,32,64]{4,3,2,1,0:T(8,128)} custom-call(bf16[192,512]{1,0:T(8,128)(2,1)S(1)} %get-tuple-element.15.refs_0_, bf16[192,512]{1,0:T(8,128)(2,1)S(1)} %collective-permute-done.refs_1_, bf16[192,512]{1,0:T(8,128)(2,1)S(1)} %get-tuple-element.16.refs_2_, bf16[192,512]{1,0:T(8,128)(2,1)S(1)} %collective-permute-done.1.refs_3_, ...), custom_call_target="tpu_custom_call" | custom-call | tf_op jit(solution)/shard_map/weight_gradient/pallas_call | solution.py:309
  151.6 3.1 %all-to-all-done = bf16[16,48,512]{2,1,0:T(8,128)(2,1)S(1)} async-done(((bf16[16,48,512]{2,1,0:T(8,128)(2,1)}), bf16[16,48,512]{2,1,0:T(8,128)(2,1)S(1)}, u32[]{:S(2)}, u32[]{:S(2)}) %all-to-all-start) | async-done | bytes 786464 | tf_op jit(solution)/shard_map/all_to_all | solution.py:494
  154.7 13.0 %final.1 = bf16[1,4,32,64,512]{4,3,2,1,0:T(8,128)(2,1)} custom-call(bf16[4,32,64,512]{3,2,1,0:T(8,128)(2,1)} %get-tuple-element.12.grad, bf16[768,512]{1,0:T(8,128)(2,1)S(1)} %bitcast.8, bf16[512,256]{1,0:T(8,128)(2,1)S(1)} %copy-done.8, bf16[192,1024]{1,0:T(8,128)(2,1)S(1)} %copy-done.1, bf16[768,768]{1,0:T(8,128)(2,1)} %constant.31.clone.perm_t, ...), custom_call_target="tpu_custom_call" | custom-call | tf_op jit(solution)/shard_map/final/pallas_call | solution.py:441
Async XLA Ops:
  0.6 1.0 copy-start
  1.6 0.8 copy-start.13
  2.5 31.2 %copy-start.2 = (bf16[512,32]{1,0:T(8,128)(2,1)S(1)}, bf16[512,32]{1,0:T(8,128)(2,1)}, u32[]{:S(2)}) copy-start(bf16[512,32]{1,0:T(8,128)(2,1)} %constant.29.clone.refs_6_.rep.refs_5_) | copy-start | bytes 98308
  2.5 31.2 %copy-start.6 = (bf16[1,768,192]{2,1,0:T(8,128)(2,1)S(1)}, bf16[1,768,192]{2,1,0:T(8,128)(2,1)}, u32[]{:S(2)}) copy-start(bf16[1,768,192]{2,1,0:T(8,128)(2,1)} %constant.26.clone.refs_3_) | copy-start | bytes 884740
  2.5 31.2 %copy-start.7 = (bf16[1,192,768]{2,1,0:T(8,128)(2,1)S(1)}, bf16[1,192,768]{2,1,0:T(8,128)(2,1)}, u32[]{:S(2)}) copy-start(bf16[1,192,768]{2,1,0:T(8,128)(2,1)} %constant.25.clone.refs_2_) | copy-start | bytes 884740
  2.5 31.2 %copy-start.11 = (bf16[512,512]{1,0:T(8,128)(2,1)S(1)}, bf16[512,512]{1,0:T(8,128)(2,1)}, u32[]{:S(2)}) copy-start(bf16[512,512]{1,0:T(8,128)(2,1)} %constant.27.clone.refs_4_) | copy-start | bytes 1572868
  2.5 31.2 %copy-start.12 = (bf16[32,512]{1,0:T(8,128)(2,1)S(1)}, bf16[32,512]{1,0:T(8,128)(2,1)}, u32[]{:S(2)}) copy-start(bf16[32,512]{1,0:T(8,128)(2,1)} %constant.28.clone.refs_5_.refs_4_) | copy-start | bytes 98308
  32.7 0.9 copy-start.5
  33.6 35.6 %copy-start.1 = (bf16[192,1024]{1,0:T(8,128)(2,1)S(1)}, bf16[192,1024]{1,0:T(8,128)(2,1)}, u32[]{:S(2)}) copy-start(bf16[192,1024]{1,0:T(8,128)(2,1)} %constant.23.clone.inner) | copy-start | bytes 1179652
  33.6 35.6 %copy-start.8 = (bf16[512,256]{1,0:T(8,128)(2,1)S(1)}, bf16[512,256]{1,0:T(8,128)(2,1)}, u32[]{:S(2)}) copy-start(bf16[512,256]{1,0:T(8,128)(2,1)} %constant.30.clone.ys) | copy-start | bytes 786436
  33.6 35.6 %copy-start.14 = (bf16[32,32]{1,0:T(8,128)(2,1)S(1)}, bf16[32,32]{1,0:T(8,128)(2,1)}, u32[]{:S(2)}) copy-start(bf16[32,32]{1,0:T(8,128)(2,1)} %point.3) | copy-start | bytes 6148
  33.6 35.6 %copy-start.15 = (f32[32]{0:T(128)S(1)}, f32[32]{0:T(128)}, u32[]{:S(2)}) copy-start(f32[32]{0:T(128)} %bias.1) | copy-start | bytes 388
  44.6 1.1 copy-start.9
  68.3 0.9 copy-start.3
  69.2 48.8 %copy-start.10 = (bf16[512,512]{1,0:T(8,128)(2,1)S(1)}, bf16[512,512]{1,0:T(8,128)(2,1)}, u32[]{:S(2)}) copy-start(bf16[512,512]{1,0:T(8,128)(2,1)} %constant.32.clone.refs_4_) | copy-start | bytes 1572868
  117.1 0.9 copy-start.4
  130.9 23.8 %all-to-all-start = ((bf16[16,48,512]{2,1,0:T(8,128)(2,1)}), bf16[16,48,512]{2,1,0:T(8,128)(2,1)S(1)}, u32[]{:S(2)}, u32[]{:S(2)}) async-start(bf16[16,48,512]{2,1,0:T(8,128)(2,1)} %bitcast.15), calls=%async_computation | async-start | bytes 1572864 | tf_op jit(solution)/shard_map/all_to_all | solution.py:494
  136.2 1.5 collective-permute-start
  136.2 1.7 %collective-permute-start.1 = (bf16[192,512]{1,0:T(8,128)(2,1)S(1)}, bf16[192,512]{1,0:T(8,128)(2,1)S(1)}, u32[]{:S(2)}, u32[]{:S(2)}) collective-permute-start(bf16[192,512]{1,0:T(8,128)(2,1)S(1)} %get-tuple-element.16.refs_2_), channel_id=1, source_target_pairs={{0,1},{1,0},{2,3},{3,2},{4,5},{5,4},{6,7},{7,6},{8,9},{9,8},{10,11... | collective-permute-start | bytes 589832 | tf_op jit(solution)/shard_map/ppermute | solution.py:500
